TPU v7x, 128 devices: a whole 4x4x4 slice. The times are simulated.
128 devices in a mesh: outer: 4 (over z_lo, core), inner: 32 (over y, z_hi, x).
Axes of the slice: x: 4, y: 4, z: 4 (z_hi: 2, z_lo: 2; z = z_hi * 2 + z_lo), core: 2. Of those that a mesh axis runs over, the one named last changes fastest.
Arguments:
- coefficients: float32 [2, 5, 5, 128, 4096], P(None, None, None, ('outer', 'inner')), may hold values from -2.5 to 2.5
- speed_amp: float32 [8], replicated, may hold values from -0.12 to 0.12
- speed_wave: float32 [2, 8], replicated, may hold values from -24 to 24
- speed_shift: float32 [8], replicated, may hold values from -3.140625 to 3.140625
Outputs:
- transformed: float32 [2, 5, 5, 524288], P(None, None, None, ('outer', 'inner'))
All inputs are finite; a program needn't handle non-finite values.
Results may differ from a plain program's by a relative error of at most 0.003.
Values sent between devices are 32-bit elements; how exact they have to be, the bound alone decides.
No kernel may reach another device: no remote copies, remote signals or barrier semaphores. Data moves between devices by JAX's collectives and lax.ppermute only.
A program may use at most 192 MiB of HBM per device.

v0:
```python
import math

import jax
import jax.numpy as jnp
import numpy as np
from jax import lax
from jax.sharding import PartitionSpec as P

N = 16384
CHEB = 5
MODES = 8
TX = 32
TY = 128


TWO_PI = 2.0 * math.pi


def from_partner(value, axis, apart):
    mask = 2**apart
    pairs = [(source, source ^ mask) for source in range(lax.axis_size(axis))]
    return lax.ppermute(value, axis, pairs)


def split_first(level_idx, total_bits):
    return (total_bits - 1 - level_idx) % 2 == 0


def box_widths(level_idx, total_bits):
    splits_x = sum((1 for bit_pos in range(total_bits) if split_first(bit_pos, total_bits)))
    splits_y = total_bits - splits_x
    before_x = sum((1 for bit_pos in range(level_idx) if split_first(bit_pos, total_bits)))
    before_y = level_idx - before_x
    return (2.0**splits_x / N / 2.0**before_x, 2.0**splits_y / N / 2.0**before_y)


def cheb_tables():
    points = 0.5 * np.cos(np.arange(CHEB) * np.pi / (CHEB - 1))
    child_points = np.stack([(half_idx - 0.5) / 2.0 + points / 2.0 for half_idx in (0, 1)], axis=1)
    lagrange = np.ones((2, CHEB, CHEB))
    for half_idx in range(2):
        for row_idx in range(CHEB):
            for col_idx in range(CHEB):
                for other_idx in range(CHEB):
                    if other_idx != col_idx:
                        lagrange[half_idx, row_idx, col_idx] *= (
                            child_points[row_idx, half_idx] - points[other_idx]
                        ) / (points[col_idx] - points[other_idx])
    return (
        jnp.asarray(points, jnp.float32),
        jnp.asarray(child_points, jnp.float32),
        jnp.asarray(lagrange, jnp.float32),
    )


def speed_field(pos_x, pos_y, speed_params):
    speed_amp, speed_wave, speed_shift = speed_params
    summed = jnp.zeros_like(pos_x + pos_y, dtype=jnp.float32)
    for mode_idx in range(MODES):
        summed = summed + speed_amp[mode_idx] * jnp.sin(
            TWO_PI * (speed_wave[0, mode_idx] * pos_x + speed_wave[1, mode_idx] * pos_y)
            + speed_shift[mode_idx]
        )
    return summed


def source_centre(source_ids, level_idx, total_bits):
    freq_x = jnp.zeros_like(jnp.asarray(source_ids), dtype=jnp.float32)
    freq_y = jnp.zeros_like(jnp.asarray(source_ids), dtype=jnp.float32)
    for bit_pos in range(level_idx, total_bits):
        bit_sign = (source_ids // 2 ** (bit_pos - level_idx) % 2).astype(jnp.float32) - 0.5
        bit_depth = (total_bits - 1 - bit_pos) // 2 + 1
        if split_first(bit_pos, total_bits):
            freq_x = freq_x + bit_sign * (N / 2.0**bit_depth)
        else:
            freq_y = freq_y + bit_sign * (N / 2.0**bit_depth)
    return (freq_x, freq_y)


def start_centres(total_bits):
    box_index = jnp.arange(TX * TY, dtype=jnp.int32)
    width_x, width_y = box_widths(0, total_bits)
    centre_x = ((box_index // TY).astype(jnp.float32) + 0.5) * width_x
    centre_y = ((box_index % TY).astype(jnp.float32) + 0.5) * width_y
    return (centre_x, centre_y)


def expand_centres(centre_x, centre_y, level_idx, total_bits):
    width_x, width_y = box_widths(level_idx, total_bits)
    if split_first(level_idx, total_bits):
        new_x = jnp.concatenate([centre_x - 0.25 * width_x, centre_x + 0.25 * width_x], axis=-1)
        new_y = jnp.concatenate([centre_y, centre_y], axis=-1)
    else:
        new_y = jnp.concatenate([centre_y - 0.25 * width_y, centre_y + 0.25 * width_y], axis=-1)
        new_x = jnp.concatenate([centre_x, centre_x], axis=-1)
    return (new_x, new_y)


def level_tables(centre_x, centre_y, level_idx, total_bits, speed_params):
    points, child_points, lagrange = cheb_tables()
    width_x, width_y = box_widths(level_idx, total_bits)
    extra = (1,) * centre_x.ndim
    nodes_x = points.reshape((CHEB, 1) + extra)
    nodes_y = points.reshape((1, CHEB) + extra)
    off_x = width_x * nodes_x
    off_y = width_y * nodes_y
    speed_centre = speed_field(centre_x, centre_y, speed_params)
    speed_near = speed_field(centre_x + off_x, centre_y + off_y, speed_params) - speed_centre
    along_x = split_first(level_idx, total_bits)
    children = []
    for half_idx in range(2):
        if along_x:
            child_x = width_x * child_points[:, half_idx].reshape((CHEB, 1) + extra)
            child_y = off_y
        else:
            child_x = off_x
            child_y = width_y * child_points[:, half_idx].reshape((1, CHEB) + extra)
        speed_child = (
            speed_field(centre_x + child_x, centre_y + child_y, speed_params) - speed_centre
        )
        children.append((child_x, child_y, speed_child))
    return (off_x, off_y, speed_near, children, lagrange, along_x)


def branch_terms(values, centre, tables):
    freq_x, freq_y = centre
    off_x, off_y, speed_near, children, lagrange, along_x = tables
    freq_abs = jnp.sqrt(freq_x * freq_x + freq_y * freq_y)
    phase_in = TWO_PI * (off_x * freq_x + off_y * freq_y + speed_near * freq_abs)
    cos_in = jnp.cos(phase_in)
    sin_in = jnp.sin(phase_in)
    rotated = jnp.stack(
        [values[0] * cos_in + values[1] * sin_in, values[1] * cos_in - values[0] * sin_in]
    )
    results = []
    for half_idx in range(2):
        if along_x:
            interpolated = jnp.einsum(
                "ab,rbc...->rac...", lagrange[half_idx], rotated, precision=lax.Precision.HIGHEST
            )
        else:
            interpolated = jnp.einsum(
                "cb,rab...->rac...", lagrange[half_idx], rotated, precision=lax.Precision.HIGHEST
            )
        child_x, child_y, speed_child = children[half_idx]
        phase_out = TWO_PI * (child_x * freq_x + child_y * freq_y + speed_child * freq_abs)
        cos_out = jnp.cos(phase_out)
        sin_out = jnp.sin(phase_out)
        results.append(
            jnp.stack(
                [
                    interpolated[0] * cos_out - interpolated[1] * sin_out,
                    interpolated[0] * sin_out + interpolated[1] * cos_out,
                ]
            )
        )
    return results


def join_halves(left_terms, right_terms):
    return jnp.concatenate(
        [left_terms[0] + right_terms[0], left_terms[1] + right_terms[1]], axis=-1
    )


def flip_bits(number, levels):
    result = 0
    for bit_pos in range(levels):
        result = result * 2 + (number >> bit_pos & 1)
    return result


def restore_order(current, levels):
    width_all = current.shape[-1]
    halves = 2**levels
    base = width_all // halves
    flipped_ids = np.array([flip_bits(pos, levels) for pos in range(halves)], dtype=np.int32)
    view = current.reshape(current.shape[:-1] + (halves, base))
    view = jnp.take(view, jnp.asarray(flipped_ids), axis=-2)
    view = jnp.swapaxes(view, -1, -2)
    return view.reshape(current.shape[:-1] + (width_all,))


def on_device(coefficients, speed_amp, speed_wave, speed_shift):
    speed_params = (speed_amp, speed_wave, speed_shift)
    outer_count = lax.axis_size("outer")
    inner_count = lax.axis_size("inner")
    devices = outer_count * inner_count
    total_bits = devices.bit_length() - 1
    inner_bits = inner_count.bit_length() - 1
    outer_pos = lax.axis_index("outer")
    inner_pos = lax.axis_index("inner")
    device = outer_pos * inner_count + inner_pos
    per_device = coefficients.shape[4] // devices
    centre_x, centre_y = start_centres(total_bits)
    current = coefficients.reshape(2, CHEB, CHEB, devices, per_device)
    centre_x = centre_x.reshape(devices, per_device)
    centre_y = centre_y.reshape(devices, per_device)
    for level_idx in range(total_bits):
        bit_value = device // 2**level_idx % 2
        half_count = current.shape[3] // 2
        width_now = current.shape[4]
        split_view = current.reshape(2, CHEB, CHEB, half_count, 2, width_now)
        kept_half = lax.dynamic_index_in_dim(split_view, bit_value, 4, keepdims=False)
        outgoing = lax.dynamic_index_in_dim(split_view, 1 - bit_value, 4, keepdims=False)
        if level_idx < inner_bits:
            received = from_partner(outgoing, "inner", level_idx)
        else:
            received = from_partner(outgoing, "outer", level_idx - inner_bits)
        centre_x = lax.dynamic_index_in_dim(
            centre_x.reshape(half_count, 2, width_now), bit_value, 1, keepdims=False
        )
        centre_y = lax.dynamic_index_in_dim(
            centre_y.reshape(half_count, 2, width_now), bit_value, 1, keepdims=False
        )
        tables = level_tables(centre_x, centre_y, level_idx, total_bits, speed_params)
        own_source = device // 2**level_idx
        own_centre = source_centre(own_source, level_idx, total_bits)
        partner_centre = source_centre(own_source + 1 - 2 * bit_value, level_idx, total_bits)
        current = join_halves(
            branch_terms(kept_half, own_centre, tables),
            branch_terms(received, partner_centre, tables),
        )
        centre_x, centre_y = expand_centres(centre_x, centre_y, level_idx, total_bits)
    flat = current.reshape(2, CHEB, CHEB, -1)
    return restore_order(flat, total_bits)


def solution(mesh):
    in_specs = (P(None, None, None, ("outer", "inner"), None), P(), P(), P())
    out_specs = P(None, None, None, ("outer", "inner"))
    return jax.shard_map(
        on_device, mesh=mesh, in_specs=in_specs, out_specs=out_specs, check_vma=False
    )
```

profile of v0, /device:TPU:1, one launch (start us, length us, event | category | flops | bytes accessed | tf_op | source)
XLA Modules:
  0.0 964.3 jit_solution(15423949304821070420)
XLA Ops:
  20.1 20.3 %multiply_add_fusion.37 = (f32[64,32]{0,1:T(8,128)S(1)}, f32[64,1,32]{0,2,1:T(8,128)S(1)}) fusion(f32[]{:T(128)} %bitcast.34, f32[]{:T(128)} %bitcast.33, f32[]{:T(128)} %bitcast.32, f32[]{:T(128)} %bitcast.31, f32[]{:T(128)} %bitcast.30, f32[]{:T(128)} %bitcast.29, f32[]{:T(128)} %bitcast.28, f32[]{:T(128)} %bitcast.27, f32[]{:T(128)} %bitcast.26, ...), kind=kLoop, calls=%fused_computation.651 | loop fusion | flops 126976 | bytes 34948 | tf_op jit(solution)/shard_map/add | solution.py:60
  42.5 20.7 %multiply_add_fusion.41 = f32[8,256]{1,0:T(8,128)} fusion(f32[]{:T(128)} %bitcast.34, f32[]{:T(128)} %bitcast.33, f32[]{:T(128)} %bitcast.32, f32[]{:T(128)} %bitcast.31, f32[]{:T(128)} %bitcast.30, f32[]{:T(128)} %bitcast.29, f32[]{:T(128)} %bitcast.28, f32[]{:T(128)} %bitcast.27, f32[]{:T(128)} %bitcast.26, f32[]{:T(128)} %bitcast.25, f32[]{:T(128)} %bitcast.24, ...), kind=kLoop, calls=%fused_computation.682 | loop fusion | flops 112640 | bytes 24704 | tf_op jit(solution)/shard_map/add | solution.py:60
  64.5 20.9 %multiply_add_fusion.40 = f32[4,512]{1,0:T(4,128)} fusion(f32[]{:T(128)} %bitcast.34, f32[]{:T(128)} %bitcast.33, f32[]{:T(128)} %bitcast.32, f32[]{:T(128)} %bitcast.31, f32[]{:T(128)} %bitcast.30, f32[]{:T(128)} %bitcast.29, f32[]{:T(128)} %bitcast.28, f32[]{:T(128)} %bitcast.27, f32[]{:T(128)} %bitcast.26, f32[]{:T(128)} %bitcast.25, f32[]{:T(128)} %bitcast.24, ...), kind=kLoop, calls=%fused_computation.679 | loop fusion | flops 112640 | bytes 24704 | tf_op jit(solution)/shard_map/add | solution.py:60
  86.7 20.7 %multiply_add_fusion.39 = f32[2,1024]{1,0:T(2,128)S(1)} fusion(f32[]{:T(128)} %bitcast.34, f32[]{:T(128)} %bitcast.33, f32[]{:T(128)} %bitcast.32, f32[]{:T(128)} %bitcast.31, f32[]{:T(128)} %bitcast.30, f32[]{:T(128)} %bitcast.29, f32[]{:T(128)} %bitcast.28, f32[]{:T(128)} %bitcast.27, f32[]{:T(128)} %bitcast.26, f32[]{:T(128)} %bitcast.25, f32[]{:T(128)} %bitcast.24, ...), kind=kLoop, calls=%fused_computation.676 | loop fusion | flops 112640 | bytes 24704 | tf_op jit(solution)/shard_map/add | solution.py:60
  115.4 5.1 add_multiply_fusion.67
  120.5 20.9 %multiply_add_fusion.36 = f32[32,64]{1,0:T(8,128)} fusion(f32[32,64]{1,0:T(8,128)S(1)} %bitcast.457, f32[32,64]{1,0:T(8,128)S(1)} %bitcast.460, f32[]{:T(128)} %bitcast.34, f32[]{:T(128)} %bitcast.33, f32[]{:T(128)} %bitcast.32, f32[]{:T(128)} %bitcast.31, f32[]{:T(128)} %bitcast.30, f32[]{:T(128)} %bitcast.29, f32[]{:T(128)} %bitcast.28, f32[]{:T(128)} %bitcast.27, ...), kind=kLoop, calls=%fused_computation.650 | loop fusion | flops 112640 | bytes 24704 | tf_op jit(solution)/shard_map/add | solution.py:60
  141.4 5.2 add_multiply_fusion.19
  163.6 20.7 %multiply_add_fusion.42 = f32[16,128]{1,0:T(8,128)} fusion(f32[16,128]{1,0:T(8,128)S(1)} %bitcast.472, f32[16,128]{1,0:T(8,128)S(1)} %bitcast.466, f32[]{:T(128)} %bitcast.34, f32[]{:T(128)} %bitcast.33, f32[]{:T(128)} %bitcast.32, f32[]{:T(128)} %bitcast.31, f32[]{:T(128)} %bitcast.30, f32[]{:T(128)} %bitcast.29, f32[]{:T(128)} %bitcast.28, f32[]{:T(128)} %bitcast.27, ...), kind=kLoop, calls=%fused_computation.683 | loop fusion | flops 112640 | bytes 24704 | tf_op jit(solution)/shard_map/add | solution.py:60
  184.3 5.8 add_multiply_fusion.257
  190.2 5.1 add_multiply_fusion.225
  195.9 5.8 add_multiply_fusion.249
  216.5 5.8 add_multiply_fusion.265
  222.3 5.9 add_multiply_fusion.169
  228.2 22.5 %multiply_add_fusion.38 = (f32[1,2048]{1,0:T(1,128)}, f32[1,2048]{1,0:T(1,128)}, f32[1,2048]{1,0:T(1,128)}) fusion(f32[]{:T(128)} %bitcast.34, f32[]{:T(128)} %bitcast.33, f32[]{:T(128)} %bitcast.32, f32[]{:T(128)} %bitcast.31, f32[]{:T(128)} %bitcast.30, f32[]{:T(128)} %bitcast.29, f32[]{:T(128)} %bitcast.28, f32[]{:T(128)} %bitcast.27, f32[]{:T(128)} %bitcast.26, ...), kind=kLoop, calls=%fused_computation.675 | loop fusion | flops 116736 | bytes 49284 | tf_op jit(solution)/shard_map/add | solution.py:60
  258.7 6.0 add_multiply_fusion.51
  264.7 23.7 %multiply_add_fusion.8 = (f32[1,5,5,64,32]{3,4,2,1,0:T(8,128)S(1)}, f32[1,5,5,64,32]{3,4,2,1,0:T(8,128)S(1)}) fusion(f32[2,5,5,64,32]{3,4,2,1,0:T(8,128)} %collective-permute-done, f32[]{:T(128)S(6)} %sqrt.43, f32[5,5]{1,0:T(8,128)S(1)} %get-tuple-element.606, f32[64,32]{0,1:T(8,128)S(1)} %get-tuple-element.66, f32[]{:T(128)} %bitcast.34, ...), kind=kLoop, calls=%fused_computation.171 | loop fusion | flops 2355200 | bytes 1482920 | tf_op jit(solution)/shard_map/add | solution.py:133
  302.8 22.7 %multiply_subtract_fusion.7 = (f32[1,5,5,64,32]{3,4,2,1,0:T(8,128)S(1)}, f32[1,5,5,64,32]{3,4,2,1,0:T(8,128)S(1)}) fusion(f32[2,5,5,64,32]{3,4,2,1,0:T(8,128)S(1)} %bitcast.400, f32[5,5]{1,0:T(8,128)S(1)} %get-tuple-element.605, f32[]{:T(128)S(6)} %sqrt.43, f32[64,32]{0,1:T(8,128)S(1)} %get-tuple-element.66, f32[]{:T(128)} %bitcast.34, ...), kind=kLoop, calls=%fused_computation.168 | loop fusion | flops 2355200 | bytes 1482920 | tf_op jit(solution)/shard_map/sub | solution.py:152
  341.0 22.6 %multiply_subtract_fusion.5 = (f32[1,5,5,64,32]{3,4,2,1,0:T(8,128)S(1)}, f32[1,5,5,64,32]{3,4,2,1,0:T(8,128)S(1)}) fusion(f32[2,5,5,64,32]{3,4,2,1,0:T(8,128)S(1)} %bitcast.398, f32[5,5]{1,0:T(8,128)S(1)} %copy-done.173, f32[]{:T(128)S(6)} %sqrt.43, f32[64,32]{0,1:T(8,128)S(1)} %get-tuple-element.66, f32[]{:T(128)} %bitcast.34, ...), kind=kLoop, calls=%fused_computation.161 | loop fusion | flops 2355200 | bytes 1482920 | tf_op jit(solution)/shard_map/sub | solution.py:152
  384.2 5.1 add_multiply_fusion.43
  389.3 12.0 %collective-permute-done.1 = f32[2,5,5,32,64]{4,3,2,1,0:T(8,128)S(1)} collective-permute-done((f32[2,5,5,32,64]{4,3,2,1,0:T(8,128)S(1)}, f32[2,5,5,32,64]{4,3,2,1,0:T(8,128)S(1)}, u32[]{:S(2)}, u32[]{:S(2)}) %collective-permute-start.1) | collective-permute-done | bytes 409632 | tf_op jit(solution)/shard_map/ppermute | solution.py:22
  401.5 30.2 %fusion.10 = (f32[1,5,5,32,64]{4,2,3,1,0:T(8,128)S(1)}, f32[1,5,5,32,64]{4,2,3,1,0:T(8,128)S(1)}) fusion(f32[1,5,5,32,64]{4,3,2,1,0:T(8,128)S(1)} %get-tuple-element.125, f32[1,5,5,32,64]{4,3,2,1,0:T(8,128)S(1)} %get-tuple-element.124, f32[]{:T(128)S(6)} %sqrt.45, f32[5,5]{1,0:T(8,128)S(1)} %copy-done.174, f32[32,64]{1,0:T(8,128)S(1)} %copy-done.83, ...), kind=kLoop, calls=%fused_computation.73 | loop fusion | flops 2355200 | bytes 1482920 | tf_op jit(solution)/shard_map/add | solution.py:133
  431.7 5.6 multiply_add_fusion.4
  442.7 30.3 %multiply_subtract_fusion.2 = (f32[1,5,5,32,64]{4,2,3,1,0:T(8,128)S(1)}, f32[1,5,5,32,64]{4,2,3,1,0:T(8,128)S(1)}) fusion(f32[2,5,5,32,64]{4,2,3,1,0:T(8,128)S(1)} %convolution_bitcast_fusion.2, f32[5,5]{1,0:T(8,128)S(1)} %copy-done.176, f32[]{:T(128)S(6)} %sqrt.45, f32[32,64]{1,0:T(8,128)S(1)} %copy-done.83, f32[]{:T(128)} %bitcast.34, ...), kind=kLoop, calls=%fused_computation.119 | loop fusion | flops 2355200 | bytes 1482920 | tf_op jit(solution)/shard_map/sub | solution.py:152
  473.1 5.4 multiply_subtract_fusion.3
  480.3 29.9 %multiply_subtract_fusion = (f32[1,5,5,32,64]{4,2,3,1,0:T(8,128)S(1)}, f32[1,5,5,32,64]{4,2,3,1,0:T(8,128)S(1)}) fusion(f32[2,5,5,32,64]{4,2,3,1,0:T(8,128)S(1)} %convolution_bitcast_fusion, f32[5,5]{1,0:T(8,128)S(1)} %copy-done.175, f32[]{:T(128)S(6)} %sqrt.45, f32[32,64]{1,0:T(8,128)S(1)} %copy-done.83, f32[]{:T(128)} %bitcast.34, ...), kind=kLoop, calls=%fused_computation.112 | loop fusion | flops 2355200 | bytes 1482920 | tf_op jit(solution)/shard_map/sub | solution.py:152
  510.3 5.7 multiply_subtract_fusion.1
  522.7 5.2 add_multiply_fusion.201
  530.0 19.9 %fusion.56 = (f32[1,5,5,16,128]{4,1,3,2,0:T(8,128)S(1)}, f32[1,5,5,16,128]{4,1,3,2,0:T(8,128)S(1)}) fusion(f32[1,5,5,16,128]{4,3,2,1,0:T(8,128)S(1)} %get-tuple-element.138, f32[1,5,5,16,128]{4,3,2,1,0:T(8,128)S(1)} %get-tuple-element.137, f32[]{:T(128)S(6)} %sqrt.47, f32[5,5]{0,1:T(8,128)S(1)} %copy-done.172, f32[16,128]{1,0:T(8,128)S(1)} %copy-done.149, ...), kind=kLoop, calls=%fused_computation.275 | loop fusion | flops 2355200 | bytes 1482920 | tf_op jit(solution)/shard_map/add | solution.py:133
  556.0 20.3 %multiply_subtract_fusion.32 = (f32[1,5,5,16,128]{4,1,3,2,0:T(8,128)S(1)}, f32[1,5,5,16,128]{4,1,3,2,0:T(8,128)S(1)}) fusion(f32[2,5,5,16,128]{4,1,3,2,0:T(8,128)S(1)} %convolution_bitcast_fusion.18, f32[5,5]{0,1:T(8,128)S(1)} %copy-done.171, f32[]{:T(128)S(6)} %sqrt.47, f32[16,128]{1,0:T(8,128)S(1)} %copy-done.149, f32[]{:T(128)} %bitcast.34, ...), kind=kLoop, calls=%fused_computation.377 | loop fusion | flops 2355200 | bytes 1482920 | tf_op jit(solution)/shard_map/sub | solution.py:152
  579.8 19.9 %multiply_subtract_fusion.30 = (f32[1,5,5,16,128]{4,1,3,2,0:T(8,128)S(1)}, f32[1,5,5,16,128]{4,1,3,2,0:T(8,128)S(1)}) fusion(f32[2,5,5,16,128]{4,1,3,2,0:T(8,128)S(1)} %convolution_bitcast_fusion.16, f32[5,5]{0,1:T(8,128)S(1)} %copy-done.169, f32[]{:T(128)S(6)} %sqrt.47, f32[16,128]{1,0:T(8,128)S(1)} %copy-done.149, f32[]{:T(128)} %bitcast.34, ...), kind=kLoop, calls=%fused_computation.370 | loop fusion | flops 2355200 | bytes 1482920 | tf_op jit(solution)/shard_map/sub | solution.py:152
  606.2 6.3 add_multiply_fusion.177
  612.9 19.9 %fusion.58 = (f32[1,5,5,8,256]{4,2,3,1,0:T(8,128)S(1)}, f32[1,5,5,8,256]{4,2,3,1,0:T(8,128)S(1)}) fusion(f32[1,5,5,8,256]{4,3,2,1,0:T(8,128)S(1)} %get-tuple-element.136, f32[1,5,5,8,256]{4,3,2,1,0:T(8,128)S(1)} %get-tuple-element.135, f32[]{:T(128)S(6)} %sqrt.49, f32[5,5]{1,0:T(8,128)S(1)} %copy-done.167, f32[8,256]{1,0:T(8,128)S(1)} %copy-done.148, ...), kind=kLoop, calls=%fused_computation.277 | loop fusion | flops 2355200 | bytes 1482920 | tf_op jit(solution)/shard_map/add | solution.py:133
  639.2 19.9 %multiply_subtract_fusion.27 = (f32[1,5,5,8,256]{4,2,3,1,0:T(8,128)S(1)}, f32[1,5,5,8,256]{4,2,3,1,0:T(8,128)S(1)}) fusion(f32[2,5,5,8,256]{4,2,3,1,0:T(8,128)S(1)} %convolution_bitcast_fusion.14, f32[5,5]{1,0:T(8,128)S(1)} %copy-done.166, f32[]{:T(128)S(6)} %sqrt.49, f32[8,256]{1,0:T(8,128)S(1)} %copy-done.148, f32[]{:T(128)} %bitcast.34, ...), kind=kLoop, calls=%fused_computation.358 | loop fusion | flops 2355200 | bytes 1482920 | tf_op jit(solution)/shard_map/sub | solution.py:152
  663.2 19.9 %multiply_subtract_fusion.25 = (f32[1,5,5,8,256]{4,2,3,1,0:T(8,128)S(1)}, f32[1,5,5,8,256]{4,2,3,1,0:T(8,128)S(1)}) fusion(f32[2,5,5,8,256]{4,2,3,1,0:T(8,128)S(1)} %convolution_bitcast_fusion.12, f32[5,5]{1,0:T(8,128)S(1)} %copy-done.164, f32[]{:T(128)S(6)} %sqrt.49, f32[8,256]{1,0:T(8,128)S(1)} %copy-done.148, f32[]{:T(128)} %bitcast.34, ...), kind=kLoop, calls=%fused_computation.351 | loop fusion | flops 2355200 | bytes 1482920 | tf_op jit(solution)/shard_map/sub | solution.py:152
  694.2 5.2 add_multiply_fusion.145
  699.6 20.8 %fusion.60 = (f32[1,5,5,4,512]{4,1,3,2,0:T(8,128)S(1)}, f32[1,5,5,4,512]{4,1,3,2,0:T(8,128)S(1)}) fusion(f32[1,5,5,4,512]{4,3,2,1,0:T(4,128)S(1)} %get-tuple-element.134, f32[1,5,5,4,512]{4,3,2,1,0:T(4,128)S(1)} %get-tuple-element.133, f32[]{:T(128)S(6)} %sqrt.51, f32[5,5]{0,1:T(8,128)S(1)} %copy-done.165, f32[4,512]{1,0:T(4,128)S(1)} %copy-done.147, ...), kind=kLoop, calls=%fused_computation.279 | loop fusion | flops 2355200 | bytes 1482920 | tf_op jit(solution)/shard_map/add | solution.py:133
  726.8 20.3 %multiply_subtract_fusion.22 = (f32[1,5,5,4,512]{4,1,3,2,0:T(8,128)S(1)}, f32[1,5,5,4,512]{4,1,3,2,0:T(8,128)S(1)}) fusion(f32[2,5,5,4,512]{4,1,3,2,0:T(8,128)S(1)} %convolution_bitcast_fusion.10, f32[5,5]{0,1:T(8,128)S(1)} %copy-done.163, f32[]{:T(128)S(6)} %sqrt.51, f32[4,512]{1,0:T(4,128)S(1)} %copy-done.147, f32[]{:T(128)} %bitcast.34, ...), kind=kLoop, calls=%fused_computation.339 | loop fusion | flops 2355200 | bytes 1482920 | tf_op jit(solution)/shard_map/sub | solution.py:152
  751.0 19.9 %multiply_subtract_fusion.20 = (f32[1,5,5,4,512]{4,1,3,2,0:T(8,128)S(1)}, f32[1,5,5,4,512]{4,1,3,2,0:T(8,128)S(1)}) fusion(f32[2,5,5,4,512]{4,1,3,2,0:T(8,128)S(1)} %convolution_bitcast_fusion.8, f32[5,5]{0,1:T(8,128)S(1)} %copy-done.162, f32[]{:T(128)S(6)} %sqrt.51, f32[4,512]{1,0:T(4,128)S(1)} %copy-done.147, f32[]{:T(128)} %bitcast.34, ...), kind=kLoop, calls=%fused_computation.332 | loop fusion | flops 2355200 | bytes 1482920 | tf_op jit(solution)/shard_map/sub | solution.py:152
  779.2 5.2 add_multiply_fusion.121
  784.5 19.9 %fusion.62 = (f32[1,5,5,2,1024]{4,2,3,1,0:T(8,128)S(1)}, f32[1,5,5,2,1024]{4,2,3,1,0:T(8,128)S(1)}) fusion(f32[1,5,5,2,1024]{4,3,2,1,0:T(2,128)S(1)} %get-tuple-element.132, f32[1,5,5,2,1024]{4,3,2,1,0:T(2,128)S(1)} %get-tuple-element.131, f32[]{:T(128)S(6)} %sqrt.53, f32[5,5]{1,0:T(8,128)S(1)} %copy-done.170, f32[2,1024]{1,0:T(2,128)S(1)} %multiply_add_fusion.39, ...), kind=kLoop, calls=%fused_computation.281 | loop fusion | flops 2355200 | bytes 1482920 | tf_op jit(solution)/shard_map/add | solution.py:133
  810.7 20.0 %multiply_subtract_fusion.17 = (f32[1,5,5,2,1024]{4,2,3,1,0:T(8,128)S(1)}, f32[1,5,5,2,1024]{4,2,3,1,0:T(8,128)S(1)}) fusion(f32[2,5,5,2,1024]{4,2,3,1,0:T(8,128)S(1)} %convolution_bitcast_fusion.6, f32[5,5]{1,0:T(8,128)S(1)} %copy-done.168, f32[]{:T(128)S(6)} %sqrt.53, f32[2,1024]{1,0:T(2,128)S(1)} %multiply_add_fusion.39, f32[]{:T(128)} %bitcast.34, ...), kind=kLoop, calls=%fused_computation.320 | loop fusion | flops 2355200 | bytes 1482920 | tf_op jit(solution)/shard_map/sub | solution.py:152
  833.6 19.9 %multiply_subtract_fusion.15 = (f32[1,5,5,2,1024]{4,2,3,1,0:T(8,128)S(1)}, f32[1,5,5,2,1024]{4,2,3,1,0:T(8,128)S(1)}) fusion(f32[2,5,5,2,1024]{4,2,3,1,0:T(8,128)S(1)} %convolution_bitcast_fusion.4, f32[5,5]{1,0:T(8,128)S(1)} %get-tuple-element.574, f32[]{:T(128)S(6)} %sqrt.53, f32[2,1024]{1,0:T(2,128)S(1)} %multiply_add_fusion.39, f32[]{:T(128)} %bitcast.34, ...), kind=kLoop, calls=%fused_computation.313 | loop fusion | flops 2355200 | bytes 1482920 | tf_op jit(solution)/shard_map/sub | solution.py:152
  858.5 5.1 add_multiply_fusion.129
  863.5 5.2 collective-permute-done.6
  869.1 19.9 %fusion.64 = (f32[1,5,5,1,2048]{4,2,3,1,0:T(8,128)S(1)}, f32[1,5,5,1,2048]{4,2,3,1,0:T(8,128)S(1)}) fusion(f32[1,5,5,1,2048]{4,0,3,2,1:T(1,128)S(1)} %get-tuple-element.130, f32[1,5,5,1,2048]{4,0,3,2,1:T(1,128)S(1)} %get-tuple-element.129, f32[]{:T(128)S(6)} %sqrt.55, f32[5,5]{1,0:T(8,128)S(1)} %copy-done.161, f32[2048]{0:T(1024)S(1)} %bitcast.463, ...), kind=kLoop, calls=%fused_computation.283 | loop fusion | flops 2355200 | bytes 1482920 | tf_op jit(solution)/shard_map/add | solution.py:133
  897.2 20.3 %multiply_subtract_fusion.10 = (f32[1,5,5,1,2048]{4,2,3,1,0:T(8,128)S(1)}, f32[1,5,5,1,2048]{4,2,3,1,0:T(8,128)S(1)}) fusion(f32[2,5,5,1,2048]{4,2,3,1,0:T(8,128)S(1)} %bitcast.404, f32[5,5]{1,0:T(8,128)S(1)} %copy-done.160, f32[]{:T(128)S(6)} %sqrt.55, f32[2048]{0:T(1024)S(1)} %bitcast.464, f32[]{:T(128)} %bitcast.34, ...), kind=kLoop, calls=%fused_computation.294 | loop fusion | flops 2355200 | bytes 1482920 | tf_op jit(solution)/shard_map/sub | solution.py:152
  920.4 19.9 %multiply_subtract_fusion.12 = (f32[1,5,5,1,2048]{4,2,3,1,0:T(8,128)S(1)}, f32[1,5,5,1,2048]{4,2,3,1,0:T(8,128)S(1)}) fusion(f32[2,5,5,1,2048]{4,2,3,1,0:T(8,128)S(1)} %bitcast.402, f32[5,5]{1,0:T(8,128)S(1)} %copy-done.159, f32[]{:T(128)S(6)} %sqrt.55, f32[2048]{0:T(1024)S(1)} %bitcast.465, f32[]{:T(128)} %bitcast.34, ...), kind=kLoop, calls=%fused_computation.301 | loop fusion | flops 2355200 | bytes 1482920 | tf_op jit(solution)/shard_map/sub | solution.py:152
  951.2 7.6 gather_fusion
  (776 shorter events, 233.0 us)
Async XLA Ops:
  14.0 250.6 %collective-permute-start = (f32[2,5,5,64,32]{3,4,2,1,0:T(8,128)}, f32[2,5,5,64,32]{3,4,2,1,0:T(8,128)}, u32[]{:S(2)}, u32[]{:S(2)}) collective-permute-start(f32[2,5,5,64,32]{3,4,2,1,0:T(8,128)} %bitcast.450), channel_id=1, source_target_pairs={{0,1},{1,0},{2,3},{3,2},{4,5},{5,4},{6,7},{7,6},{8,9},{9,8},{10,11... | collective-permute-start | bytes 1228808 | tf_op jit(solution)/shard_map/ppermute | solution.py:22
  40.4 70.6 %copy-start.145 = (f32[64,1,32]{0,2,1:T(8,128)}, f32[64,1,32]{0,2,1:T(8,128)S(1)}, u32[]{:S(2)}) copy-start(f32[64,1,32]{0,2,1:T(8,128)S(1)} %get-tuple-element.67) | copy-start | bytes 24580
  41.5 69.5 %copy-start.142 = (f32[32,1,64]{2,1,0:T(1,128)}, f32[32,1,64]{2,1,0:T(1,128)S(1)}, u32[]{:S(2)}) copy-start(f32[32,1,64]{2,1,0:T(1,128)S(1)} %fusion.136) | copy-start | bytes 24580
  41.6 121.9 %copy-start.151 = (f32[16,1,128]{2,1,0:T(1,128)}, f32[16,1,128]{2,1,0:T(1,128)S(1)}, u32[]{:S(2)}) copy-start(f32[16,1,128]{2,1,0:T(1,128)S(1)} %get-tuple-element.43) | copy-start | bytes 24580
  41.8 44.3 %copy-start.155 = (f32[16,1,128]{2,1,0:T(1,128)}, f32[16,1,128]{2,1,0:T(1,128)S(1)}, u32[]{:S(2)}) copy-start(f32[16,1,128]{2,1,0:T(1,128)S(1)} %fusion.147) | copy-start | bytes 24580
  86.1 25.0 %copy-start.153 = (f32[2,1,1024]{2,1,0:T(1,128)}, f32[2,1,1024]{2,1,0:T(1,128)S(1)}, u32[]{:S(2)}) copy-start(f32[2,1,1024]{2,1,0:T(1,128)S(1)} %fusion.141) | copy-start | bytes 24580
  113.9 27.5 %copy-start.240 = (f32[5]{0:T(128)S(1)}, f32[5]{0:T(128)}, u32[]{:S(2)}) copy-start(f32[5]{0:T(128)} %constant.1072) | copy-start | bytes 64
  114.0 27.5 %copy-start.242 = (f32[5]{0:T(128)S(1)}, f32[5]{0:T(128)}, u32[]{:S(2)}) copy-start(f32[5]{0:T(128)} %constant.1070) | copy-start | bytes 64
  120.5 144.2 %copy-start.9 = (f32[5,64,32]{1,2,0:T(8,128)}, f32[5,64,32]{1,2,0:T(8,128)S(1)}, u32[]{:S(2)}) copy-start(f32[5,64,32]{1,2,0:T(8,128)S(1)} %get-tuple-element.219) | copy-start | bytes 122884
  120.5 144.2 %copy-start.12 = (f32[5,64,32]{1,2,0:T(8,128)}, f32[5,64,32]{1,2,0:T(8,128)S(1)}, u32[]{:S(2)}) copy-start(f32[5,64,32]{1,2,0:T(8,128)S(1)} %get-tuple-element.220) | copy-start | bytes 122884
  155.0 29.2 %copy-start.211 = (f32[5]{0:T(128)S(1)}, f32[5]{0:T(128)}, u32[]{:S(2)}) copy-start(f32[5]{0:T(128)} %constant.1073) | copy-start | bytes 64
  156.5 33.7 %copy-start.178 = (f32[8,1,256]{2,0,1:T(8,128)S(1)}, f32[8,1,256]{2,0,1:T(8,128)}, u32[]{:S(2)}) copy-start(f32[8,1,256]{2,0,1:T(8,128)} %copy.808) | copy-start | bytes 24580
  156.5 33.7 %copy-start.219 = (f32[5]{0:T(128)S(1)}, f32[5]{0:T(128)}, u32[]{:S(2)}) copy-start(f32[5]{0:T(128)} %constant.1077) | copy-start | bytes 64
  156.5 33.7 %copy-start.221 = (f32[5]{0:T(128)S(1)}, f32[5]{0:T(128)}, u32[]{:S(2)}) copy-start(f32[5]{0:T(128)} %constant.1075) | copy-start | bytes 64
  160.0 35.9 %copy-start.181 = (f32[8,1,256]{2,0,1:T(8,128)S(1)}, f32[8,1,256]{2,0,1:T(8,128)}, u32[]{:S(2)}) copy-start(f32[8,1,256]{2,0,1:T(8,128)} %copy.809) | copy-start | bytes 24580
  206.2 21.9 %copy-start.185 = (f32[2,1024]{1,0:T(2,128)S(1)}, f32[2,1024]{1,0:T(2,128)}, u32[]{:S(2)}) copy-start(f32[2,1024]{1,0:T(2,128)} %get-tuple-element.429) | copy-start | bytes 24580
  206.3 21.9 %copy-start.186 = (f32[2,1024]{1,0:T(2,128)S(1)}, f32[2,1024]{1,0:T(2,128)}, u32[]{:S(2)}) copy-start(f32[2,1024]{1,0:T(2,128)} %get-tuple-element.430) | copy-start | bytes 24580
  206.9 43.8 %copy-start.223 = (f32[5]{0:T(128)S(1)}, f32[5]{0:T(128)}, u32[]{:S(2)}) copy-start(f32[5]{0:T(128)} %constant.1046.clone) | copy-start | bytes 64
  206.9 44.4 %copy-start.247 = (f32[5,1]{0,1:T(1,128)S(1)}, f32[5,1]{0,1:T(1,128)}, u32[]{:S(2)}) copy-start(f32[5,1]{0,1:T(1,128)} %constant.1066) | copy-start | bytes 64
  206.9 44.4 %copy-start.248 = (f32[5,1]{0,1:T(1,128)S(1)}, f32[5,1]{0,1:T(1,128)}, u32[]{:S(2)}) copy-start(f32[5,1]{0,1:T(1,128)} %constant.1061) | copy-start | bytes 64
  208.2 49.1 %copy-start.245 = (f32[5]{0:T(128)S(1)}, f32[5]{0:T(128)}, u32[]{:S(2)}) copy-start(f32[5]{0:T(128)} %constant.1083) | copy-start | bytes 64
  208.2 50.5 %copy-start.85 = (f32[64,1,32]{0,2,1:T(8,128)S(1)}, f32[64,1,32]{0,2,1:T(8,128)}, u32[]{:S(2)}) copy-start(f32[64,1,32]{0,2,1:T(8,128)} %copy-done.84) | copy-start | bytes 24580
  208.2 50.5 %copy-start.249 = (f32[5]{0:T(128)S(1)}, f32[5]{0:T(128)}, u32[]{:S(2)}) copy-start(f32[5]{0:T(128)} %constant.1068) | copy-start | bytes 64
  208.2 50.5 %copy-start.250 = (f32[5]{0:T(128)S(1)}, f32[5]{0:T(128)}, u32[]{:S(2)}) copy-start(f32[5]{0:T(128)} %constant.1063) | copy-start | bytes 64
  208.2 50.5 %copy-start.251 = (f32[5]{0:T(128)S(1)}, f32[5]{0:T(128)}, u32[]{:S(2)}) copy-start(f32[5]{0:T(128)} %constant.1057) | copy-start | bytes 64
  341.0 22.6 %copy-start.204 = (f32[5,5]{1,0:T(8,128)S(1)}, f32[5,5]{1,0:T(8,128)}, u32[]{:S(2)}) copy-start(f32[5,5]{1,0:T(8,128)} %get-tuple-element.601) | copy-start | bytes 304
  380.4 21.0 %copy-start.51 = (f32[5,32,64]{2,0,1:T(8,128)S(1)}, f32[5,32,64]{2,0,1:T(8,128)}, u32[]{:S(2)}) copy-start(f32[5,32,64]{2,0,1:T(8,128)} %copy.525) | copy-start | bytes 122884
  380.4 21.0 %copy-start.52 = (f32[5,32,64]{2,0,1:T(8,128)S(1)}, f32[5,32,64]{2,0,1:T(8,128)}, u32[]{:S(2)}) copy-start(f32[5,32,64]{2,0,1:T(8,128)} %copy.524) | copy-start | bytes 122884
  380.4 21.0 %copy-start.53 = (f32[5,32,64]{2,0,1:T(8,128)S(1)}, f32[5,32,64]{2,0,1:T(8,128)}, u32[]{:S(2)}) copy-start(f32[5,32,64]{2,0,1:T(8,128)} %copy.523) | copy-start | bytes 122884
  380.4 21.0 %copy-start.54 = (f32[5,32,64]{2,0,1:T(8,128)S(1)}, f32[5,32,64]{2,0,1:T(8,128)}, u32[]{:S(2)}) copy-start(f32[5,32,64]{2,0,1:T(8,128)} %copy.522) | copy-start | bytes 122884
  380.4 21.0 %copy-start.55 = (f32[5,32,64]{2,0,1:T(8,128)S(1)}, f32[5,32,64]{2,0,1:T(8,128)}, u32[]{:S(2)}) copy-start(f32[5,32,64]{2,0,1:T(8,128)} %copy.521) | copy-start | bytes 122884
  380.4 21.0 %copy-start.56 = (f32[5,32,64]{2,0,1:T(8,128)S(1)}, f32[5,32,64]{2,0,1:T(8,128)}, u32[]{:S(2)}) copy-start(f32[5,32,64]{2,0,1:T(8,128)} %copy.520) | copy-start | bytes 122884
  380.4 21.0 %copy-start.57 = (f32[5,32,64]{2,0,1:T(8,128)S(1)}, f32[5,32,64]{2,0,1:T(8,128)}, u32[]{:S(2)}) copy-start(f32[5,32,64]{2,0,1:T(8,128)} %copy.519) | copy-start | bytes 122884
  380.4 21.0 %copy-start.58 = (f32[5,32,64]{2,0,1:T(8,128)S(1)}, f32[5,32,64]{2,0,1:T(8,128)}, u32[]{:S(2)}) copy-start(f32[5,32,64]{2,0,1:T(8,128)} %copy.518) | copy-start | bytes 122884
  380.5 21.0 %copy-start.83 = (f32[32,64]{1,0:T(8,128)S(1)}, f32[32,64]{1,0:T(8,128)}, u32[]{:S(2)}) copy-start(f32[32,64]{1,0:T(8,128)} %multiply_add_fusion.36) | copy-start | bytes 24580
  380.5 21.0 %copy-start.174 = (f32[5,5]{1,0:T(8,128)S(1)}, f32[5,5]{1,0:T(8,128)}, u32[]{:S(2)}) copy-start(f32[5,5]{1,0:T(8,128)} %get-tuple-element.600) | copy-start | bytes 304
  380.5 20.8 %collective-permute-start.1 = (f32[2,5,5,32,64]{4,3,2,1,0:T(8,128)S(1)}, f32[2,5,5,32,64]{4,3,2,1,0:T(8,128)S(1)}, u32[]{:S(2)}, u32[]{:S(2)}) collective-permute-start(f32[2,5,5,32,64]{4,3,2,1,0:T(8,128)S(1)} %bitcast.451), channel_id=1, source_target_pairs={{0,2},{1,3},{2,0},{3,1},{4,6},{5,7},{6,4},{7,5},{8,10},{9,11},{10,... | collective-permute-start | bytes 1228808 | tf_op jit(solution)/shard_map/ppermute | solution.py:22
  401.5 30.2 %copy-start.207 = (f32[5,5]{1,0:T(8,128)S(1)}, f32[5,5]{1,0:T(8,128)}, u32[]{:S(2)}) copy-start(f32[5,5]{1,0:T(8,128)} %get-tuple-element.597) | copy-start | bytes 304
  442.7 30.3 %copy-start.206 = (f32[5,5]{1,0:T(8,128)S(1)}, f32[5,5]{1,0:T(8,128)}, u32[]{:S(2)}) copy-start(f32[5,5]{1,0:T(8,128)} %get-tuple-element.596) | copy-start | bytes 304
  480.3 29.9 %copy-start.205 = (f32[5,5]{1,0:T(8,128)S(1)}, f32[5,5]{1,0:T(8,128)}, u32[]{:S(2)}) copy-start(f32[5,5]{1,0:T(8,128)} %get-tuple-element.595) | copy-start | bytes 304
  518.3 11.6 %collective-permute-start.2 = (f32[2,5,5,16,128]{4,3,2,1,0:T(8,128)S(1)}, f32[2,5,5,16,128]{4,3,2,1,0:T(8,128)S(1)}, u32[]{:S(2)}, u32[]{:S(2)}) collective-permute-start(f32[2,5,5,16,128]{4,3,2,1,0:T(8,128)S(1)} %bitcast.454), channel_id=1, source_target_pairs={{0,4},{1,5},{2,6},{3,7},{4,0},{5,1},{6,2},{7,3},{8,12},{9,13},{10,... | collective-permute-start | bytes 1228808 | tf_op jit(solution)/shard_map/ppermute | solution.py:22
  527.9 22.0 %copy-start.200 = (f32[5,5]{0,1:T(8,128)S(1)}, f32[5,5]{0,1:T(8,128)}, u32[]{:S(2)}) copy-start(f32[5,5]{0,1:T(8,128)} %get-tuple-element.591) | copy-start | bytes 304
  604.1 8.5 collective-permute-start.3
  687.4 12.0 %collective-permute-start.4 = (f32[2,5,5,4,512]{4,3,2,1,0:T(4,128)S(1)}, f32[2,5,5,4,512]{4,3,2,1,0:T(4,128)S(1)}, u32[]{:S(2)}, u32[]{:S(2)}) collective-permute-start(f32[2,5,5,4,512]{4,3,2,1,0:T(4,128)S(1)} %bitcast.452), channel_id=1, source_target_pairs={{0,16},{1,17},{2,18},{3,19},{4,20},{5,21},{6,22},{7,23},{8,24},{9,... | collective-permute-start | bytes 1228808 | tf_op jit(solution)/shard_map/ppermute | solution.py:22
  699.4 21.0 %copy-start.198 = (f32[5,5]{0,1:T(8,128)S(1)}, f32[5,5]{0,1:T(8,128)}, u32[]{:S(2)}) copy-start(f32[5,5]{0,1:T(8,128)} %get-tuple-element.579) | copy-start | bytes 304
  775.4 9.1 collective-permute-start.5
  857.2 11.5 %collective-permute-start.6 = (f32[2,5,5,1,2048]{4,0,3,2,1:T(2,128)S(1)}, f32[2,5,5,1,2048]{4,0,3,2,1:T(2,128)S(1)}, u32[]{:S(2)}, u32[]{:S(2)}) collective-permute-start(f32[2,5,5,1,2048]{4,0,3,2,1:T(2,128)S(1)} %copy.623), channel_id=1, source_target_pairs={{0,64},{32,96},{64,0},{96,32},{1,65},{33,97},{65,1},{97,33},{2,66}... | collective-permute-start | bytes 1228808 | tf_op jit(solution)/shard_map/ppermute | solution.py:22
  863.5 25.5 %copy-start.191 = (f32[5,5]{1,0:T(8,128)S(1)}, f32[5,5]{1,0:T(8,128)}, u32[]{:S(2)}) copy-start(f32[5,5]{1,0:T(8,128)} %get-tuple-element.516) | copy-start | bytes 304
  (211 other events, 1078.5 us)
where the time goes:
time: 976 us; the launch traced here: 964 us
  other arithmetic  779 us (80%)
  local copies, waits for them, and re-layouts  113 us (12%)
  matrix products  27.7 us (3%)
  waiting for transfers between devices  19.4 us (2%)
  starting transfers between devices  18.9 us (2%)
    sub x28, other arithmetic, branch_terms(): interpolated[0] * cos_out - interpolated[1] * sin_out  354 us
    add x14, other arithmetic, branch_terms(): values[0] * cos_in + values[1] * sin_in  181 us
    add x7, other arithmetic, speed_field(): summed + speed_amp[mode_idx] * jnp.sin(TWO_PI * (speed_wave[0, mode_idx]...  147 us
    mul x7, other arithmetic, speed_field(): speed_wave[0, mode_idx] * pos_x + speed_wave[1, mode_idx] * pos_y  39.5 us
    mul x7, other arithmetic, speed_field(): speed_wave[1, mode_idx] * pos_y  37.2 us
    mul x48, local copies, waits for them, and re-layouts, speed_field(): speed_wave[1, mode_idx] * pos_y  32.1 us
  transfers between devices with their start and end apart: 7, of which 4 were waited for; matrix products, arithmetic and copies ran while one was open for 29% of the time, Pallas kernels for 0%

commit v1 on v0

v1 whole, which is shorter than its diff:
```python
import math

import jax
import jax.numpy as jnp
import numpy as np
from jax import lax
from jax.experimental import pallas as pl
from jax.experimental.pallas import tpu as pltpu
from jax.sharding import PartitionSpec as P

N = 16384
CHEB = 5
MODES = 8
TX = 32
TY = 128
BITS = 7
DEVICES = 128
LANES = 128
NODES = CHEB * CHEB
PLANES = 2 * NODES
LOW = TX * TY // DEVICES
HALF = LOW // 2
PACK = LANES // LOW
PACKED = -(-PLANES // PACK)
LANE_BIT = (0, 1, 2, 3, 4, 5, 6)
LEVEL_TABLE = 8 * NODES
TABLE = 25
FIRST_ROW = BITS * TABLE
OFFSET_ROW = FIRST_ROW + 1 + 2 * CHEB
TWO_PI = 2.0 * math.pi
ROUND = 1.5 * 2.0**23
AXES = ("outer", "inner")


def split_first(level):
    return (BITS - 1 - level) % 2 == 0


def box_widths(level):
    splits_x = sum(1 for bit in range(BITS) if split_first(bit))
    splits_y = BITS - splits_x
    before_x = sum(1 for bit in range(level) if split_first(bit))
    before_y = level - before_x
    return (2.0**splits_x / N / 2.0**before_x, 2.0**splits_y / N / 2.0**before_y)


def points_of():
    points = 0.5 * np.cos(np.arange(CHEB) * np.pi / (CHEB - 1))
    child = np.stack([(half - 0.5) / 2.0 + points / 2.0 for half in (0, 1)])
    return points, child


def lagrange_of(u):
    points, _ = points_of()
    row = np.ones(CHEB)
    for j in range(CHEB):
        for m in range(CHEB):
            if m != j:
                row[j] *= (u - points[m]) / (points[j] - points[m])
    return row


def source_centre(ids, level):
    freq_x = np.zeros(len(ids))
    freq_y = np.zeros(len(ids))
    for bit in range(level, BITS):
        sign = (ids >> bit) % 2 - 0.5
        depth = (BITS - 1 - bit) // 2 + 1
        if split_first(bit):
            freq_x = freq_x + sign * (N / 2.0**depth)
        else:
            freq_y = freq_y + sign * (N / 2.0**depth)
    return freq_x, freq_y


def lane_tables():
    points, child = points_of()
    lane = np.arange(LANES)
    bit_of = [(lane >> LANE_BIT[k]) % 2 for k in range(BITS)]
    rows = []
    for level in range(BITS):
        width = box_widths(level)[0 if split_first(level) else 1]
        parent_id = sum(bit_of[k] << k for k in range(level + 1, BITS)) + 0 * lane
        parent_x, parent_y = source_centre(parent_id, level + 1)
        parent = np.sqrt(parent_x**2 + parent_y**2)
        centres = [source_centre(parent_id + (c << level), level) for c in range(2)]
        move_x = np.zeros(LANES)
        move_y = (lane % 2) * (HALF * box_widths(0)[1])
        for k in range(level):
            wide_x, wide_y = box_widths(k)
            half = (bit_of[k + 1] - 0.5) / 2.0
            if split_first(k):
                move_x = move_x + half * wide_x
            else:
                move_y = move_y + half * wide_y
        for c in range(2):
            rows.append(np.sqrt(centres[c][0] ** 2 + centres[c][1] ** 2) - parent)
        rows += [parent, move_x, move_y]
        for c in range(2):
            own_d, parent_d = (
                (centres[c][0], parent_x) if split_first(level) else (centres[c][1], parent_y)
            )
            for half in range(2):
                for i in range(CHEB):
                    turn = width * child[half, i] * own_d - width * points[i] / 2.0 * parent_d
                    rows.append(turn - np.round(turn))
    source = sum(bit_of[k] << k for k in range(BITS))
    freq_x, freq_y = source_centre(source, 0)
    wide_x, wide_y = box_widths(0)
    rows.append(-np.sqrt(freq_x**2 + freq_y**2))
    for i in range(CHEB):
        turn = -wide_x * points[i] * freq_x
        rows.append(turn - np.round(turn))
    for j in range(CHEB):
        turn = -wide_y * points[j] * freq_y
        rows.append(turn - np.round(turn))
    off_x, off_y = offset_tables()
    for level in range(BITS + 1):
        rows += [off_x[level], off_y[level]]
    while len(rows) % 8:
        rows.append(np.zeros(LANES))
    return np.stack(rows).astype(np.float32)


def offset_tables():
    points, child = points_of()
    off_x = np.zeros((BITS + 1, LANES))
    off_y = np.zeros((BITS + 1, LANES))
    for level in range(BITS + 1):
        wide_x, wide_y = box_widths(level % BITS)
        for a in range(CHEB):
            for b in range(CHEB):
                p = a * CHEB + b
                if level == BITS:
                    off_x[level, p], off_y[level, p] = wide_x * points[a], wide_y * points[b]
                elif split_first(level):
                    off_x[level, p], off_y[level, p] = wide_x * child[0, a], wide_y * points[b]
                else:
                    off_x[level, p], off_y[level, p] = wide_x * points[b], wide_y * child[0, a]
    return off_x, off_y


def chebyshev_fit(function, odd, terms):
    grid = 0.5 * np.cos((np.arange(400) + 0.5) * np.pi / 400)
    powers = np.stack([grid ** (2 * k + (1 if odd else 0)) for k in range(terms)], axis=1)
    answer, *_ = np.linalg.lstsq(powers, function(TWO_PI * grid), rcond=None)
    return [float(v) for v in answer]


SIN_FIT = chebyshev_fit(np.sin, True, 7)
COS_FIT = chebyshev_fit(np.cos, False, 7)


def horner(fit, square):
    total = fit[-1]
    for value in fit[-2::-1]:
        total = total * square + value
    return total


def sin_cos(turns):
    turns = turns - ((turns + ROUND) - ROUND)
    square = turns * turns
    return turns * horner(SIN_FIT, square), horner(COS_FIT, square)


def swap(left, right, shift, low):
    first = jnp.where(low, left, pltpu.roll(right, shift, 1))
    second = jnp.where(low, pltpu.roll(left, LANES - shift, 1), right)
    return first, second


def in_hbm(value):
    return pltpu.with_memory_space_constraint(value, pltpu.HBM)


def pack_kernel(rows_hbm, out_ref, in_ref, sems):
    rows = DEVICES // PACK
    lane = lax.broadcasted_iota(jnp.int32, (rows, LANES), 1)
    low64 = lane < 2 * LOW
    low32 = lane % (2 * LOW) < LOW
    copies = []
    for m in range(PACKED):
        start = PACK * m * rows
        size = min(PACK * rows, PLANES * rows - start)
        copies.append(
            pltpu.make_async_copy(
                rows_hbm.at[pl.ds(start, size)], in_ref.at[pl.ds(start, size)], sems.at[m]
            )
        )
        copies[m].start()
    for m in range(PACKED):
        copies[m].wait()
        blocks = []
        for n in range(PACK):
            plane = min(PACK * m + n, PLANES - 1)
            blocks.append(in_ref[plane * rows : (plane + 1) * rows, :])
        blocks[0], blocks[2] = swap(blocks[0], blocks[2], 2 * LOW, low64)
        blocks[1], blocks[3] = swap(blocks[1], blocks[3], 2 * LOW, low64)
        blocks[0], blocks[1] = swap(blocks[0], blocks[1], LOW, low32)
        blocks[2], blocks[3] = swap(blocks[2], blocks[3], LOW, low32)
        for r in range(PACK):
            out_ref[pl.ds(r * PACKED + m, rows, stride=PACK * PACKED), :] = blocks[r]


def pack(rows_in):
    return pl.pallas_call(
        pack_kernel,
        in_specs=[pl.BlockSpec(memory_space=pltpu.HBM)],
        out_specs=pl.BlockSpec(memory_space=pltpu.VMEM),
        out_shape=jax.ShapeDtypeStruct((DEVICES * PACKED, LANES), jnp.float32),
        scratch_shapes=[
            pltpu.VMEM((PLANES * DEVICES // PACK, LANES), jnp.float32),
            pltpu.SemaphoreType.DMA((PACKED,)),
        ],
        compiler_params=pltpu.CompilerParams(vmem_limit_bytes=16 * 2**20),
        cost_estimate=pl.CostEstimate(flops=10**6, bytes_accessed=1700000, transcendentals=0),
    )(in_hbm(rows_in))


def phase_kernel(
    amp_hbm,
    speed_hbm,
    shift_hbm,
    lane_hbm,
    table_hbm,
    first_hbm,
    amp_ref,
    speed_ref,
    shift_ref,
    lane_ref,
    table_ref,
    first_ref,
    row_ref,
    wave_ref,
    mode_ref,
    mode_smem,
    sems,
    out_sems,
):
    fetches = [
        pltpu.make_async_copy(source, target, sems.at[k])
        for k, (source, target) in enumerate(
            (
                (amp_hbm, amp_ref),
                (speed_hbm, speed_ref),
                (shift_hbm, shift_ref),
                (lane_hbm, lane_ref),
            )
        )
    ]
    for fetch in fetches:
        fetch.start()
    for fetch in fetches:
        fetch.wait()
    device = lax.axis_index(AXES)
    wide_x, wide_y = box_widths(0)
    per_row = TY // LOW
    base_x = (device // per_row).astype(jnp.float32) * wide_x + 0.5 * wide_x
    base_y = (device % per_row).astype(jnp.float32) * (LOW * wide_y) + 0.5 * wide_y

    which = lax.broadcasted_iota(jnp.int32, (MODES, LANES), 0)
    kx = jnp.zeros((MODES, LANES), jnp.float32)
    ky = jnp.zeros((MODES, LANES), jnp.float32)
    for mode in range(MODES):
        kx = jnp.where(which == mode, speed_ref[0, mode], kx)
        ky = jnp.where(which == mode, speed_ref[1, mode], ky)
    for level in range(BITS + 1):
        at = OFFSET_ROW + 2 * level
        turns = kx * lane_ref[at : at + 1, :] + ky * lane_ref[at + 1 : at + 2, :]
        half = 0.5 * turns
        half = half * horner(SIN_FIT, half * half)
        at = level * 2 * MODES
        mode_ref[at : at + MODES, :] = -2.0 * half * half
        mode_ref[at + MODES : at + 2 * MODES, :] = turns * horner(SIN_FIT, turns * turns)
    copy = pltpu.make_async_copy(mode_ref, mode_smem, sems.at[4])
    copy.start()

    low = lax.broadcasted_iota(jnp.int32, (LOW, LANES), 0).astype(jnp.float32) * wide_y
    for mode in range(MODES):
        at_base = (
            speed_ref[0, mode] * base_x
            + speed_ref[1, mode] * base_y
            + shift_ref[mode] * (1.0 / TWO_PI)
        )
        sine, cosine = sin_cos(at_base + speed_ref[1, mode] * low)
        row_ref[mode] = amp_ref[mode] * sine
        row_ref[MODES + mode] = amp_ref[mode] * cosine
    copy.wait()

    def differences(source_ref, level, p, groups):
        even = [None] * groups
        odd = [None] * groups
        for mode in range(MODES):
            less = mode_smem[level * 2 * MODES + mode, p]
            sine = mode_smem[level * 2 * MODES + MODES + mode, p]
            for t in range(groups):
                rows = slice(8 * t, 8 * t + 8)
                x = source_ref[mode, rows, :] * less
                y = source_ref[MODES + mode, rows, :] * sine
                even[t] = x if mode == 0 else even[t] + x
                odd[t] = y if mode == 0 else odd[t] + y
        return [(even[t] + odd[t], even[t] - odd[t]) for t in range(groups)]

    def put(ref, at, rows, turns):
        sine, cosine = sin_cos(turns)
        ref[at, rows, :] = cosine
        ref[at + 1, rows, :] = sine

    length = lane_ref[FIRST_ROW : FIRST_ROW + 1, :]

    def first_step(p, carry):
        a = p // CHEB
        b = p - a * CHEB
        line = (
            lane_ref[pl.ds(FIRST_ROW + 1 + a, 1), :]
            + lane_ref[pl.ds(FIRST_ROW + 1 + CHEB + b, 1), :]
        )
        back = (
            lane_ref[pl.ds(FIRST_ROW + CHEB - a, 1), :]
            + lane_ref[pl.ds(FIRST_ROW + 2 * CHEB - b, 1), :]
        )
        for t, (here, there) in enumerate(differences(row_ref, BITS, p, LOW // 8)):
            rows = slice(8 * t, 8 * t + 8)
            put(first_ref, 2 * p, rows, here * length + line)
            put(first_ref, 2 * (NODES - 1 - p), rows, there * length + back)
        return carry

    lax.fori_loop(0, NODES // 2 + 1, first_step, 0)
    first_copy = pltpu.make_async_copy(first_ref, first_hbm, sems.at[5])
    first_copy.start()

    def table_copy(level):
        part = pl.ds(level * LEVEL_TABLE, LEVEL_TABLE)
        return pltpu.make_async_copy(
            table_ref.at[part], table_hbm.at[part], out_sems.at[level]
        )

    def level_step(level, carry):
        top = level * TABLE
        apart = [lane_ref[pl.ds(top + c, 1), :] for c in range(2)]
        parent = lane_ref[pl.ds(top + 2, 1), :]
        move_x = lane_ref[pl.ds(top + 3, 1), :]
        move_y = lane_ref[pl.ds(top + 4, 1), :]
        for mode in range(MODES):
            sine, cosine = sin_cos(speed_ref[0, mode] * move_x + speed_ref[1, mode] * move_y)
            old_sine = row_ref[mode, :HALF, :]
            old_cosine = row_ref[MODES + mode, :HALF, :]
            wave_ref[mode] = old_sine * cosine + old_cosine * sine
            wave_ref[MODES + mode] = old_cosine * cosine - old_sine * sine
        moved = [
            (here * parent, there * parent)
            for here, there in differences(wave_ref, level, NODES // 2, HALF // 8)
        ]

        def pair_step(p, inner_carry):
            a = p // CHEB
            far = differences(wave_ref, level, p, HALF // 8)
            for c in range(2):
                line = lane_ref[pl.ds(top + 5 + 2 * CHEB * c + a, 1), :]
                back = lane_ref[pl.ds(top + 5 + 2 * CHEB * (c + 1) - 1 - a, 1), :]
                at = (2 * level + c) * (4 * NODES)
                for t in range(HALF // 8):
                    rows = slice(8 * t, 8 * t + 8)
                    put(table_ref, at + 2 * p, rows, far[t][0] * apart[c] + (moved[t][0] + line))
                    put(
                        table_ref,
                        at + 2 * (2 * NODES - 1 - p),
                        rows,
                        far[t][1] * apart[c] + (moved[t][1] + back),
                    )
            return inner_carry

        lax.fori_loop(0, NODES, pair_step, 0)
        table_copy(level).start()
        return carry

    lax.fori_loop(0, BITS, level_step, 0)
    first_copy.wait()
    for level in range(BITS):
        table_copy(level).wait()


def phases(speed_amp, speed_wave, speed_shift, lanes):
    return pl.pallas_call(
        phase_kernel,
        in_specs=[pl.BlockSpec(memory_space=pltpu.HBM)] * 4,
        out_specs=[pl.BlockSpec(memory_space=pltpu.HBM)] * 2,
        out_shape=[
            pltpu.HBM((BITS * LEVEL_TABLE, HALF, LANES), jnp.float32),
            pltpu.HBM((2 * NODES, LOW, LANES), jnp.float32),
        ],
        scratch_shapes=[
            pltpu.SMEM((MODES,), jnp.float32),
            pltpu.SMEM((2, MODES), jnp.float32),
            pltpu.SMEM((MODES,), jnp.float32),
            pltpu.VMEM(lanes.shape, jnp.float32),
            pltpu.VMEM((BITS * LEVEL_TABLE, HALF, LANES), jnp.float32),
            pltpu.VMEM((2 * NODES, LOW, LANES), jnp.float32),
            pltpu.VMEM((2 * MODES, LOW, LANES), jnp.float32),
            pltpu.VMEM((2 * MODES, HALF, LANES), jnp.float32),
            pltpu.VMEM(((BITS + 1) * 2 * MODES, LANES), jnp.float32),
            pltpu.SMEM(((BITS + 1) * 2 * MODES, LANES), jnp.float32),
            pltpu.SemaphoreType.DMA((6,)),
            pltpu.SemaphoreType.DMA((BITS,)),
        ],
        compiler_params=pltpu.CompilerParams(vmem_limit_bytes=32 * 2**20),
        cost_estimate=pl.CostEstimate(
            flops=70 * 10**6, bytes_accessed=13 * 10**6, transcendentals=3 * 10**6
        ),
    )(*map(in_hbm, (speed_amp, speed_wave, speed_shift, lanes)))


def interpolate(values):
    _, child = points_of()
    even0, odd0 = values[0] + values[4], values[0] - values[4]
    even1, odd1 = values[1] + values[3], values[1] - values[3]
    first = [values[2], None, None, None, values[4]]
    second = [values[0], None, None, None, values[2]]
    for i in range(1, CHEB - 1):
        row = lagrange_of(child[0, i])
        even = (
            float((row[0] + row[4]) / 2) * even0
            + float((row[1] + row[3]) / 2) * even1
            + float(row[2]) * values[2]
        )
        odd = float((row[0] - row[4]) / 2) * odd0 + float((row[1] - row[3]) / 2) * odd1
        first[i] = even + odd
        second[CHEB - 1 - i] = even - odd
    return first, second


def level_kernel(
    got_ref, table_hbm, first_hbm, out_ref, state_ref, table_ref, first_ref, sems
):
    copies = [pltpu.make_async_copy(first_hbm, first_ref, sems.at[BITS])]
    for level in range(BITS):
        part = pl.ds(level * LEVEL_TABLE, LEVEL_TABLE)
        copies.append(
            pltpu.make_async_copy(table_hbm.at[part], table_ref.at[part], sems.at[level])
        )
    for copy in copies:
        copy.start()
    for m in range(PACKED):
        block = got_ref[pl.ds(m, DEVICES, stride=PACKED), :].T
        for n in range(PACK):
            if PACK * m + n < PLANES:
                at = (PACK * m + n) * LOW
                state_ref[at : at + LOW, :] = block[n * LOW : (n + 1) * LOW, :]
    lane = lax.broadcasted_iota(jnp.int32, (8, LANES), 1)
    order = lane % 2
    for bit in range(1, BITS):
        order = order + ((lane >> (BITS - bit)) % 2 << bit)

    def line(level, b, t, places):
        shift = 2 ** LANE_BIT[level]
        low = lane // shift % 2 == 0
        sides = [[], []]
        for at in places:
            pair = []
            for half in range(2):
                row = half * HALF + 8 * t
                re = state_ref[pl.ds(at * LOW + row, 8), :]
                im = state_ref[pl.ds((NODES + at) * LOW + row, 8), :]
                if level == 0:
                    rows = slice(row, row + 8)
                    cosine, sine = first_ref[2 * at, rows, :], first_ref[2 * at + 1, rows, :]
                    re, im = re * cosine - im * sine, re * sine + im * cosine
                pair.append((re, im))
            re = swap(pair[0][0], pair[1][0], shift, low)
            im = swap(pair[0][1], pair[1][1], shift, low)
            for c in range(2):
                sides[c].append((re[c], im[c]))
        rows = slice(8 * t, 8 * t + 8)
        near = [
            [interpolate([value[r] for value in sides[c]]) for r in range(2)] for c in range(2)
        ]
        for a, at in enumerate(places):
            totals = []
            for half in range(2):
                real = imag = None
                for c in range(2):
                    e = 2 * (((2 * level + c) * 2 + half) * NODES + a * CHEB + b)
                    cosine, sine = table_ref[e, rows, :], table_ref[e + 1, rows, :]
                    re, im = near[c][0][half][a], near[c][1][half][a]
                    new_re, new_im = re * cosine - im * sine, re * sine + im * cosine
                    real = new_re if c == 0 else real + new_re
                    imag = new_im if c == 0 else imag + new_im
                totals.append((real, imag))
            for r in range(2):
                first, second = totals[0][r], totals[1][r]
                if level == BITS - 1:
                    first, second = swap(first, second, 1, lane % 2 == 0)
                    for half, value in enumerate((first, second)):
                        at_row = (at * LOW + half * HALF + 8 * t) * 2 + r
                        out_ref[pl.ds(at_row, 8, stride=2), :] = jnp.take_along_axis(
                            value, order, axis=1
                        )
                    continue
                at_row = (r * NODES + at) * LOW + 8 * t
                state_ref[pl.ds(at_row, 8), :] = first
                state_ref[pl.ds(at_row + HALF, 8), :] = second

    copies[0].wait()
    for level in range(BITS):
        copies[1 + level].wait()

        def step(b, carry, level=level):
            places = [
                a * CHEB + b if split_first(level) else b * CHEB + a for a in range(CHEB)
            ]
            for t in range(HALF // 8):
                line(level, b, t, places)
            return carry

        lax.fori_loop(0, CHEB, step, 0)


def levels(got, table, first):
    return pl.pallas_call(
        level_kernel,
        in_specs=[
            pl.BlockSpec(memory_space=pltpu.VMEM),
            pl.BlockSpec(memory_space=pltpu.HBM),
            pl.BlockSpec(memory_space=pltpu.HBM),
        ],
        out_specs=pl.BlockSpec(memory_space=pltpu.VMEM),
        out_shape=jax.ShapeDtypeStruct((PLANES * LOW, LANES), jnp.float32),
        scratch_shapes=[
            pltpu.VMEM((PLANES * LOW, LANES), jnp.float32),
            pltpu.VMEM((BITS * LEVEL_TABLE, HALF, LANES), jnp.float32),
            pltpu.VMEM((2 * NODES, LOW, LANES), jnp.float32),
            pltpu.SemaphoreType.DMA((BITS + 1,)),
        ],
        compiler_params=pltpu.CompilerParams(vmem_limit_bytes=32 * 2**20),
        cost_estimate=pl.CostEstimate(
            flops=22 * 10**6, bytes_accessed=14 * 10**6, transcendentals=0
        ),
    )(got, in_hbm(table), in_hbm(first))


def on_device(coefficients, speed_amp, speed_wave, speed_shift):
    packed = pack(coefficients.reshape(PLANES * (DEVICES // PACK), LANES))
    sent = packed.reshape(DEVICES, 1, PACKED * LANES)
    got = lax.all_to_all(sent, AXES, 0, 0, tiled=True)
    got = got.reshape(DEVICES * PACKED, LANES)
    table, first = phases(speed_amp, speed_wave, speed_shift, jnp.asarray(lane_tables()))
    final = levels(got, table, first).reshape(CHEB, CHEB, LOW, 2, LANES)
    return final.transpose(3, 0, 1, 2, 4).reshape(2, CHEB, CHEB, LOW * LANES)


def solution(mesh):
    in_specs = (P(None, None, None, AXES, None), P(), P(), P())
    out_specs = P(None, None, None, AXES)
    return jax.shard_map(
        on_device, mesh=mesh, in_specs=in_specs, out_specs=out_specs, check_vma=False
    )
```

time: 976 us -> 42.3 us (0.04); the launches traced: 964 us -> 42.1 us
  other arithmetic: 779 us -> 0 us
  local copies, waits for them, and re-layouts: 113 us -> 0 us
  Pallas kernels: 0 us -> 30.6 us
  matrix products: 27.7 us -> 0 us
  waiting for transfers between devices: 19.4 us -> 0.01 us
    sub x32 -> x0, other arithmetic: 354 us -> none  [the longest x28 354 us: branch_terms(): interpolated[0] * cos_out - interpolated[1] * sin_out]
    add x53 -> x0, other arithmetic: 342 us -> none  [the longest x14 181 us: branch_terms(): values[0] * cos_in + values[1] * sin_in]
    mul x17 -> x0, other arithmetic: 78.6 us -> none  [the longest x7 39.5 us: speed_field(): speed_wave[0, mode_idx] * pos_x + speed_wave[1, mode_idx] * pos_y]
    mul x56 -> x0, local copies, waits for them, and re-layouts: 33.6 us -> none  [the longest x48 32.1 us: speed_field(): speed_wave[1, mode_idx] * pos_y]
    pallas_call x0 -> x3, Pallas kernels: none -> 30.6 us  [the longest x1 17.5 us: phases(): pl.pallas_call(phase_kernel, in_specs=[pl.BlockSpec(memory_space=pltpu.HB...]
    another operation x43 -> x0, local copies, waits for them, and re-layouts: 29 us -> none  [the longest x40 18.1 us: branch_terms(): jnp.stack([interpolated[0] * cos_out - interpolated[1] * sin_out, interpo...]
    dot_general x28 -> x0, matrix products: 27.7 us -> none  [the longest x16 16.9 us: branch_terms(): jnp.einsum('ab,rbc...->rac...', lagrange[half_idx], rotated, precision=la...]
    ppermute x7 -> x0, waiting for transfers between devices: 19.4 us -> none  [from_partner(): return lax.ppermute(value, axis, pairs)]
  transfers between devices with their start and end apart: 7 -> 1, of which waited for: 4 -> 0; matrix products, arithmetic and copies ran while one was open for 29% -> 0% of each run, Pallas kernels for 0% -> 42%
where the time goes in v1:
time: 42.3 us; the launch traced here: 42.1 us
  Pallas kernels  30.6 us (72%)
  starting transfers between devices  11.5 us (27%)
    pallas_call x1, Pallas kernels, phases(): pl.pallas_call(phase_kernel, in_specs=[pl.BlockSpec(memory_space=pltpu.HB...  17.5 us
    all_to_all x1, starting transfers between devices, on_device(): got = lax.all_to_all(sent, AXES, 0, 0, tiled=True)  11.5 us
    pallas_call x1, Pallas kernels, levels(): pl.pallas_call(level_kernel, in_specs=[pl.BlockSpec(memory_space=pltpu.VM...  9.13 us
    pallas_call x1, Pallas kernels, pack(): pl.pallas_call(pack_kernel, in_specs=[pl.BlockSpec(memory_space=pltpu.HBM...  3.94 us
  transfers between devices with their start and end apart: 1, of which 0 were waited for; matrix products, arithmetic and copies ran while one was open for 0% of the time, Pallas kernels for 42%

profile of v1, /device:TPU:1, one launch (start us, length us, event | category | flops | bytes accessed | tf_op | source)
XLA Modules:
  0.0 42.1 jit_solution(11650676415690001339)
XLA Ops:
  0.0 3.9 %shard_map.55 = f32[1664,128]{1,0:T(8,128)} custom-call(f32[1600,128]{1,0:T(8,128)} %bitcast.9), custom_call_target="tpu_custom_call" | custom-call | flops 1000000 | bytes 1700000 | tf_op jit(solution)/shard_map/pallas_call | solution.py:207
  4.0 11.5 %all-to-all-start = ((f32[128,1,1664]{2,1,0:T(1,128)}), f32[128,1,1664]{2,1,0:T(1,128)S(1)}, u32[]{:S(2)}, u32[]{:S(2)}) async-start(f32[128,1,1664]{2,1,0:T(1,128)} %bitcast.1), calls=%async_computation | async-start | bytes 1703936 | tf_op jit(solution)/shard_map/all_to_all | solution.py:545
  15.5 17.5 %shard_map.56 = (f32[1400,16,128]{2,1,0:T(8,128)}, f32[50,32,128]{2,1,0:T(8,128)}) custom-call(f32[8]{0:T(128)} %amp_hbm.1, f32[2,8]{1,0:T(2,128)} %speed_hbm.1, f32[8]{0:T(128)} %shift_hbm.1, f32[208,128]{1,0:T(8,128)} %constant.2.clone.lane_hbm), custom_call_target="tpu_custom_call" | custom-call | flops 70000000 | bytes 13000000 | tf_op jit(solution)/shard_map/pallas_call | solution.py:385
  33.0 0.0 all-to-all-done
  33.0 9.1 %shard_map.57 = f32[1600,128]{1,0:T(8,128)} custom-call(f32[1664,128]{1,0:T(8,128)S(1)} %bitcast.8, f32[1400,16,128]{2,1,0:T(8,128)} %get-tuple-element.7.table_hbm, f32[50,32,128]{2,1,0:T(8,128)} %get-tuple-element.8.first_hbm), custom_call_target="tpu_custom_call" | custom-call | flops 22000000 | bytes 14000000 | tf_op jit(solution)/shard_map/pallas_call | solution.py:520
Async XLA Ops:
  4.0 29.0 %all-to-all-start = ((f32[128,1,1664]{2,1,0:T(1,128)}), f32[128,1,1664]{2,1,0:T(1,128)S(1)}, u32[]{:S(2)}, u32[]{:S(2)}) async-start(f32[128,1,1664]{2,1,0:T(1,128)} %bitcast.1), calls=%async_computation | async-start | bytes 1703936 | tf_op jit(solution)/shard_map/all_to_all | solution.py:545

commit v2 on v1

--- a/solution.py
+++ b/solution.py
@@ -143,12 +143,14 @@
 def chebyshev_fit(function, odd, terms):
     grid = 0.5 * np.cos((np.arange(400) + 0.5) * np.pi / 400)
     powers = np.stack([grid ** (2 * k + (1 if odd else 0)) for k in range(terms)], axis=1)
-    answer, *_ = np.linalg.lstsq(powers, function(TWO_PI * grid), rcond=None)
+    answer, *_ = np.linalg.lstsq(powers, function(math.pi * grid), rcond=None)
     return [float(v) for v in answer]
 
 
-SIN_FIT = chebyshev_fit(np.sin, True, 7)
-COS_FIT = chebyshev_fit(np.cos, False, 7)
+SIN_FIT = chebyshev_fit(np.sin, True, 4)
+COS_FIT = chebyshev_fit(np.cos, False, 5)
+SIN_FINE = chebyshev_fit(np.sin, True, 6)
+COS_FINE = chebyshev_fit(np.cos, False, 6)
 
 
 def horner(fit, square):
@@ -158,10 +160,16 @@
     return total
 
 
-def sin_cos(turns):
+def sin_cos(turns, sin_fit=SIN_FIT, cos_fit=COS_FIT):
     turns = turns - ((turns + ROUND) - ROUND)
     square = turns * turns
-    return turns * horner(SIN_FIT, square), horner(COS_FIT, square)
+    sine = turns * horner(sin_fit, square)
+    twice = sine + sine
+    return twice * horner(cos_fit, square), 1.0 - twice * sine
+
+
+def sin_cos_fine(turns):
+    return sin_cos(turns, SIN_FINE, COS_FINE)
 
 
 def swap(left, right, shift, low):
@@ -174,48 +182,67 @@
     return pltpu.with_memory_space_constraint(value, pltpu.HBM)
 
 
-def pack_kernel(rows_hbm, out_ref, in_ref, sems):
-    rows = DEVICES // PACK
-    lane = lax.broadcasted_iota(jnp.int32, (rows, LANES), 1)
-    low64 = lane < 2 * LOW
-    low32 = lane % (2 * LOW) < LOW
-    copies = []
-    for m in range(PACKED):
-        start = PACK * m * rows
-        size = min(PACK * rows, PLANES * rows - start)
-        copies.append(
+def pack_kernel(planes_hbm, out_hbm, in_ref, out_ref, in_sems, out_sems):
+    lane = lax.broadcasted_iota(jnp.int32, (8, LANES), 1)
+    high = lane >= 2 * LOW
+    odd = lane % (2 * LOW) >= LOW
+    groups = planes_hbm.shape[1] // 8
+    size = 8 * PACK * PACKED
+    fetches, stores = [], []
+    for g in range(groups):
+        fetches.append(
             pltpu.make_async_copy(
-                rows_hbm.at[pl.ds(start, size)], in_ref.at[pl.ds(start, size)], sems.at[m]
+                planes_hbm.at[:, pl.ds(8 * g, 8), :], in_ref.at[g], in_sems.at[g]
             )
         )
-        copies[m].start()
-    for m in range(PACKED):
-        copies[m].wait()
-        blocks = []
-        for n in range(PACK):
-            plane = min(PACK * m + n, PLANES - 1)
-            blocks.append(in_ref[plane * rows : (plane + 1) * rows, :])
-        blocks[0], blocks[2] = swap(blocks[0], blocks[2], 2 * LOW, low64)
-        blocks[1], blocks[3] = swap(blocks[1], blocks[3], 2 * LOW, low64)
-        blocks[0], blocks[1] = swap(blocks[0], blocks[1], LOW, low32)
-        blocks[2], blocks[3] = swap(blocks[2], blocks[3], LOW, low32)
-        for r in range(PACK):
-            out_ref[pl.ds(r * PACKED + m, rows, stride=PACK * PACKED), :] = blocks[r]
-
-
-def pack(rows_in):
+        part = pl.ds(g * size, size)
+        stores.append(
+            pltpu.make_async_copy(out_ref.at[part], out_hbm.at[part], out_sems.at[g])
+        )
+    for fetch in fetches:
+        fetch.start()
+    for g in range(groups):
+        fetches[g].wait()
+        for m in range(PACKED):
+            blocks = [in_ref[g, min(PACK * m + n, PLANES - 1)] for n in range(PACK)]
+            blocks = [
+                pltpu.roll(block, n * LOW, 1) if n else block for n, block in enumerate(blocks)
+            ]
+            for r in range(PACK):
+                part = [blocks[(k - r) % PACK] for k in range(PACK)]
+                turned = jnp.where(
+                    high,
+                    jnp.where(odd, part[3], part[2]),
+                    jnp.where(odd, part[1], part[0]),
+                )
+                out_ref[pl.ds(g * size + r * PACKED + m, 8, stride=PACK * PACKED), :] = turned
+        stores[g].start()
+    for store in stores:
+        store.wait()
+
+
+def pack(planes):
+    groups = planes.shape[1] // 8
     return pl.pallas_call(
         pack_kernel,
         in_specs=[pl.BlockSpec(memory_space=pltpu.HBM)],
-        out_specs=pl.BlockSpec(memory_space=pltpu.VMEM),
-        out_shape=jax.ShapeDtypeStruct((DEVICES * PACKED, LANES), jnp.float32),
+        out_specs=pl.BlockSpec(memory_space=pltpu.HBM),
+        out_shape=pltpu.HBM((DEVICES * PACKED, LANES), jnp.float32),
         scratch_shapes=[
-            pltpu.VMEM((PLANES * DEVICES // PACK, LANES), jnp.float32),
-            pltpu.SemaphoreType.DMA((PACKED,)),
+            pltpu.VMEM((groups, PLANES, 8, LANES), jnp.float32),
+            pltpu.VMEM((DEVICES * PACKED, LANES), jnp.float32),
+            pltpu.SemaphoreType.DMA((groups,)),
+            pltpu.SemaphoreType.DMA((groups,)),
         ],
         compiler_params=pltpu.CompilerParams(vmem_limit_bytes=16 * 2**20),
         cost_estimate=pl.CostEstimate(flops=10**6, bytes_accessed=1700000, transcendentals=0),
-    )(in_hbm(rows_in))
+    )(in_hbm(planes))
+
+
+def tree_sum(terms):
+    while len(terms) > 1:
+        terms = [terms[k] + terms[k + 1] for k in range(0, len(terms), 2)]
+    return terms[0]
 
 
 def phase_kernel(
@@ -268,11 +295,11 @@
     for level in range(BITS + 1):
         at = OFFSET_ROW + 2 * level
         turns = kx * lane_ref[at : at + 1, :] + ky * lane_ref[at + 1 : at + 2, :]
-        half = 0.5 * turns
-        half = half * horner(SIN_FIT, half * half)
+        sine, _ = sin_cos_fine(turns)
+        half = turns * horner(SIN_FINE, turns * turns)
         at = level * 2 * MODES
         mode_ref[at : at + MODES, :] = -2.0 * half * half
-        mode_ref[at + MODES : at + 2 * MODES, :] = turns * horner(SIN_FIT, turns * turns)
+        mode_ref[at + MODES : at + 2 * MODES, :] = sine
     copy = pltpu.make_async_copy(mode_ref, mode_smem, sems.at[4])
     copy.start()
 
@@ -283,24 +310,26 @@
             + speed_ref[1, mode] * base_y
             + shift_ref[mode] * (1.0 / TWO_PI)
         )
-        sine, cosine = sin_cos(at_base + speed_ref[1, mode] * low)
+        sine, cosine = sin_cos_fine(at_base + speed_ref[1, mode] * low)
         row_ref[mode] = amp_ref[mode] * sine
         row_ref[MODES + mode] = amp_ref[mode] * cosine
     copy.wait()
 
     def differences(source_ref, level, p, groups):
-        even = [None] * groups
-        odd = [None] * groups
+        even = [[] for _ in range(groups)]
+        odd = [[] for _ in range(groups)]
         for mode in range(MODES):
             less = mode_smem[level * 2 * MODES + mode, p]
             sine = mode_smem[level * 2 * MODES + MODES + mode, p]
             for t in range(groups):
                 rows = slice(8 * t, 8 * t + 8)
-                x = source_ref[mode, rows, :] * less
-                y = source_ref[MODES + mode, rows, :] * sine
-                even[t] = x if mode == 0 else even[t] + x
-                odd[t] = y if mode == 0 else odd[t] + y
-        return [(even[t] + odd[t], even[t] - odd[t]) for t in range(groups)]
+                even[t].append(source_ref[mode, rows, :] * less)
+                odd[t].append(source_ref[MODES + mode, rows, :] * sine)
+        sums = []
+        for t in range(groups):
+            x, y = tree_sum(even[t]), tree_sum(odd[t])
+            sums.append((x + y, x - y))
+        return tuple(sums)
 
     def put(ref, at, rows, turns):
         sine, cosine = sin_cos(turns)
@@ -343,7 +372,7 @@
         move_x = lane_ref[pl.ds(top + 3, 1), :]
         move_y = lane_ref[pl.ds(top + 4, 1), :]
         for mode in range(MODES):
-            sine, cosine = sin_cos(speed_ref[0, mode] * move_x + speed_ref[1, mode] * move_y)
+            sine, cosine = sin_cos_fine(speed_ref[0, mode] * move_x + speed_ref[1, mode] * move_y)
             old_sine = row_ref[mode, :HALF, :]
             old_cosine = row_ref[MODES + mode, :HALF, :]
             wave_ref[mode] = old_sine * cosine + old_cosine * sine
@@ -353,25 +382,27 @@
             for here, there in differences(wave_ref, level, NODES // 2, HALF // 8)
         ]
 
-        def pair_step(p, inner_carry):
-            a = p // CHEB
-            far = differences(wave_ref, level, p, HALF // 8)
-            for c in range(2):
-                line = lane_ref[pl.ds(top + 5 + 2 * CHEB * c + a, 1), :]
-                back = lane_ref[pl.ds(top + 5 + 2 * CHEB * (c + 1) - 1 - a, 1), :]
-                at = (2 * level + c) * (4 * NODES)
-                for t in range(HALF // 8):
-                    rows = slice(8 * t, 8 * t + 8)
-                    put(table_ref, at + 2 * p, rows, far[t][0] * apart[c] + (moved[t][0] + line))
-                    put(
-                        table_ref,
-                        at + 2 * (2 * NODES - 1 - p),
-                        rows,
-                        far[t][1] * apart[c] + (moved[t][1] + back),
-                    )
+        def row_step(a, inner_carry):
+            lines = [
+                (
+                    lane_ref[pl.ds(top + 5 + 2 * CHEB * c + a, 1), :],
+                    lane_ref[pl.ds(top + 5 + 2 * CHEB * (c + 1) - 1 - a, 1), :],
+                )
+                for c in range(2)
+            ]
+            for b in range(CHEB):
+                p = a * CHEB + b
+                far = differences(wave_ref, level, p, HALF // 8)
+                for c in range(2):
+                    at = (2 * level + c) * (4 * NODES)
+                    for t in range(HALF // 8):
+                        rows = slice(8 * t, 8 * t + 8)
+                        for k, place in enumerate((2 * p, 2 * (2 * NODES - 1 - p))):
+                            turns = far[t][k] * apart[c] + (moved[t][k] + lines[c][k])
+                            put(table_ref, at + place, rows, turns)
             return inner_carry
 
-        lax.fori_loop(0, NODES, pair_step, 0)
+        lax.fori_loop(0, CHEB, row_step, 0)
         table_copy(level).start()
         return carry
 
@@ -411,27 +442,20 @@
     )(*map(in_hbm, (speed_amp, speed_wave, speed_shift, lanes)))
 
 
-def interpolate(values):
-    _, child = points_of()
-    even0, odd0 = values[0] + values[4], values[0] - values[4]
-    even1, odd1 = values[1] + values[3], values[1] - values[3]
-    first = [values[2], None, None, None, values[4]]
-    second = [values[0], None, None, None, values[2]]
-    for i in range(1, CHEB - 1):
-        row = lagrange_of(child[0, i])
-        even = (
-            float((row[0] + row[4]) / 2) * even0
-            + float((row[1] + row[3]) / 2) * even1
-            + float(row[2]) * values[2]
-        )
-        odd = float((row[0] - row[4]) / 2) * odd0 + float((row[1] - row[3]) / 2) * odd1
-        first[i] = even + odd
-        second[CHEB - 1 - i] = even - odd
-    return first, second
-
-
 def level_kernel(
-    got_ref, table_hbm, first_hbm, out_ref, state_ref, table_ref, first_ref, sems
+    got_ref,
+    table_hbm,
+    first_hbm,
+    out_hbm,
+    state_ref,
+    other_ref,
+    table_ref,
+    first_ref,
+    out_ref,
+    slot0_ref,
+    slot1_ref,
+    sems,
+    out_sems,
 ):
     copies = [pltpu.make_async_copy(first_hbm, first_ref, sems.at[BITS])]
     for level in range(BITS):
@@ -441,79 +465,138 @@
         )
     for copy in copies:
         copy.start()
+    turn = lax.axis_index(AXES) % PACK
     for m in range(PACKED):
         block = got_ref[pl.ds(m, DEVICES, stride=PACKED), :].T
         for n in range(PACK):
-            if PACK * m + n < PLANES:
-                at = (PACK * m + n) * LOW
-                state_ref[at : at + LOW, :] = block[n * LOW : (n + 1) * LOW, :]
+            plane = PACK * m + lax.rem(n + PACK - turn, PACK)
+            state_ref[pl.ds(pl.multiple_of(plane * LOW, LOW), LOW), :] = block[
+                n * LOW : (n + 1) * LOW, :
+            ]
     lane = lax.broadcasted_iota(jnp.int32, (8, LANES), 1)
     order = lane % 2
     for bit in range(1, BITS):
         order = order + ((lane >> (BITS - bit)) % 2 << bit)
 
-    def line(level, b, t, places):
+    def places_of(level, b):
+        return [a * CHEB + b if split_first(level) else b * CHEB + a for a in range(CHEB)]
+
+    slots = (slot0_ref, slot1_ref)
+    states = (state_ref, other_ref)
+
+    def fetch(level, b, t):
         shift = 2 ** LANE_BIT[level]
         low = lane // shift % 2 == 0
-        sides = [[], []]
-        for at in places:
+        for a, at in enumerate(places_of(level, b)):
             pair = []
             for half in range(2):
                 row = half * HALF + 8 * t
-                re = state_ref[pl.ds(at * LOW + row, 8), :]
-                im = state_ref[pl.ds((NODES + at) * LOW + row, 8), :]
+                re = states[level % 2][pl.ds(at * LOW + row, 8), :]
+                im = states[level % 2][pl.ds((NODES + at) * LOW + row, 8), :]
                 if level == 0:
                     rows = slice(row, row + 8)
                     cosine, sine = first_ref[2 * at, rows, :], first_ref[2 * at + 1, rows, :]
                     re, im = re * cosine - im * sine, re * sine + im * cosine
                 pair.append((re, im))
-            re = swap(pair[0][0], pair[1][0], shift, low)
-            im = swap(pair[0][1], pair[1][1], shift, low)
+            for r in range(2):
+                for c, value in enumerate(swap(pair[0][r], pair[1][r], shift, low)):
+                    slots[t][(2 * a + r) * 2 + c] = value
+
+    def split(level, b, t, values):
+        rows = slice(8 * t, 8 * t + 8)
+        places = places_of(level, b)
+
+        def rotated(half, a, near):
+            real = imag = None
             for c in range(2):
-                sides[c].append((re[c], im[c]))
-        rows = slice(8 * t, 8 * t + 8)
-        near = [
-            [interpolate([value[r] for value in sides[c]]) for r in range(2)] for c in range(2)
-        ]
-        for a, at in enumerate(places):
-            totals = []
-            for half in range(2):
-                real = imag = None
-                for c in range(2):
-                    e = 2 * (((2 * level + c) * 2 + half) * NODES + a * CHEB + b)
-                    cosine, sine = table_ref[e, rows, :], table_ref[e + 1, rows, :]
-                    re, im = near[c][0][half][a], near[c][1][half][a]
-                    new_re, new_im = re * cosine - im * sine, re * sine + im * cosine
-                    real = new_re if c == 0 else real + new_re
-                    imag = new_im if c == 0 else imag + new_im
-                totals.append((real, imag))
+                e = 2 * (((2 * level + c) * 2 + half) * NODES + a * CHEB + b)
+                cosine, sine = table_ref[e, rows, :], table_ref[e + 1, rows, :]
+                re, im = near[0][c], near[1][c]
+                new_re, new_im = re * cosine - im * sine, re * sine + im * cosine
+                real = new_re if c == 0 else real + new_re
+                imag = new_im if c == 0 else imag + new_im
+            return real, imag
+
+        def keep(a, totals):
             for r in range(2):
                 first, second = totals[0][r], totals[1][r]
                 if level == BITS - 1:
                     first, second = swap(first, second, 1, lane % 2 == 0)
                     for half, value in enumerate((first, second)):
-                        at_row = (at * LOW + half * HALF + 8 * t) * 2 + r
-                        out_ref[pl.ds(at_row, 8, stride=2), :] = jnp.take_along_axis(
+                        at_row = (half * HALF + 8 * t) * 2 + r
+                        out_ref[a, b, pl.ds(at_row, 8, stride=2), :] = jnp.take_along_axis(
                             value, order, axis=1
                         )
                     continue
-                at_row = (r * NODES + at) * LOW + 8 * t
-                state_ref[pl.ds(at_row, 8), :] = first
-                state_ref[pl.ds(at_row + HALF, 8), :] = second
+                at_row = (r * NODES + places[a]) * LOW + 8 * t
+                states[1 - level % 2][pl.ds(at_row, 8), :] = first
+                states[1 - level % 2][pl.ds(at_row + HALF, 8), :] = second
+
+        ends = [[[values[a][r][c] for c in range(2)] for r in range(2)] for a in (0, 2, 4)]
+        keep(0, (rotated(0, 0, ends[1]), rotated(1, 0, ends[0])))
+        keep(4, (rotated(0, 4, ends[2]), rotated(1, 4, ends[1])))
+        parts = [
+            [
+                (
+                    values[0][r][c] + values[4][r][c],
+                    values[1][r][c] + values[3][r][c],
+                    values[0][r][c] - values[4][r][c],
+                    values[1][r][c] - values[3][r][c],
+                    values[2][r][c],
+                )
+                for c in range(2)
+            ]
+            for r in range(2)
+        ]
+        _, child = points_of()
+        held = {}
+        for i in range(1, CHEB - 1):
+            row = lagrange_of(child[0, i])
+            sums, gaps = [[], []], [[], []]
+            for r in range(2):
+                for c in range(2):
+                    even0, even1, odd0, odd1, middle = parts[r][c]
+                    even = (
+                        float((row[0] + row[4]) / 2) * even0
+                        + float((row[1] + row[3]) / 2) * even1
+                        + float(row[2]) * middle
+                    )
+                    odd = (
+                        float((row[0] - row[4]) / 2) * odd0
+                        + float((row[1] - row[3]) / 2) * odd1
+                    )
+                    sums[r].append(even + odd)
+                    gaps[r].append(even - odd)
+            held[0, i] = rotated(0, i, sums)
+            held[1, CHEB - 1 - i] = rotated(1, CHEB - 1 - i, gaps)
+            for a in range(1, CHEB - 1):
+                if (0, a) in held and (1, a) in held:
+                    keep(a, (held.pop((0, a)), held.pop((1, a))))
+
+    def out_copy(b):
+        return pltpu.make_async_copy(out_ref.at[:, b], out_hbm.at[:, b], out_sems.at[b])
 
     copies[0].wait()
     for level in range(BITS):
         copies[1 + level].wait()
+        for t in range(HALF // 8):
+            fetch(level, 0, t)
 
         def step(b, carry, level=level):
-            places = [
-                a * CHEB + b if split_first(level) else b * CHEB + a for a in range(CHEB)
-            ]
             for t in range(HALF // 8):
-                line(level, b, t, places)
+                values = [
+                    [[slots[t][(2 * a + r) * 2 + c] for c in range(2)] for r in range(2)]
+                    for a in range(CHEB)
+                ]
+                fetch(level, jnp.minimum(b + 1, CHEB - 1), t)
+                split(level, b, t, values)
+            if level == BITS - 1:
+                out_copy(b).start()
             return carry
 
         lax.fori_loop(0, CHEB, step, 0)
+    for b in range(CHEB):
+        out_copy(b).wait()
 
 
 def levels(got, table, first):
@@ -524,13 +607,18 @@
             pl.BlockSpec(memory_space=pltpu.HBM),
             pl.BlockSpec(memory_space=pltpu.HBM),
         ],
-        out_specs=pl.BlockSpec(memory_space=pltpu.VMEM),
-        out_shape=jax.ShapeDtypeStruct((PLANES * LOW, LANES), jnp.float32),
+        out_specs=pl.BlockSpec(memory_space=pltpu.HBM),
+        out_shape=pltpu.HBM((CHEB, CHEB, 2 * LOW, LANES), jnp.float32),
         scratch_shapes=[
+            pltpu.VMEM((PACK * PACKED * LOW, LANES), jnp.float32),
             pltpu.VMEM((PLANES * LOW, LANES), jnp.float32),
             pltpu.VMEM((BITS * LEVEL_TABLE, HALF, LANES), jnp.float32),
             pltpu.VMEM((2 * NODES, LOW, LANES), jnp.float32),
+            pltpu.VMEM((CHEB, CHEB, 2 * LOW, LANES), jnp.float32),
+            pltpu.VMEM((4 * CHEB, 8, LANES), jnp.float32),
+            pltpu.VMEM((4 * CHEB, 8, LANES), jnp.float32),
             pltpu.SemaphoreType.DMA((BITS + 1,)),
+            pltpu.SemaphoreType.DMA((CHEB,)),
         ],
         compiler_params=pltpu.CompilerParams(vmem_limit_bytes=32 * 2**20),
         cost_estimate=pl.CostEstimate(
@@ -540,7 +628,7 @@
 
 
 def on_device(coefficients, speed_amp, speed_wave, speed_shift):
-    packed = pack(coefficients.reshape(PLANES * (DEVICES // PACK), LANES))
+    packed = pack(coefficients.reshape(PLANES, DEVICES // PACK, LANES))
     sent = packed.reshape(DEVICES, 1, PACKED * LANES)
     got = lax.all_to_all(sent, AXES, 0, 0, tiled=True)
     got = got.reshape(DEVICES * PACKED, LANES)

time: 42.3 us -> 39.1 us (0.924)
  Pallas kernels: 30.6 us -> 23.6 us
  waiting for transfers between devices: 0.01 us -> 3.83 us
    pallas_call x1, Pallas kernels: 17.5 us -> 13.4 us  [phases(): pl.pallas_call(phase_kernel, in_specs=[pl.BlockSpec(memory_space=pltpu.HB...]
    all_to_all x1, waiting for transfers between devices: 0.01 us -> 3.83 us  [on_device(): got = lax.all_to_all(sent, AXES, 0, 0, tiled=True)]
    pallas_call x1, Pallas kernels: 3.94 us -> 2.13 us  [pack(): pl.pallas_call(pack_kernel, in_specs=[pl.BlockSpec(memory_space=pltpu.HBM...]
    pallas_call x1, Pallas kernels: 9.13 us -> 8.07 us  [levels(): pl.pallas_call(level_kernel, in_specs=[pl.BlockSpec(memory_space=pltpu.VM...]
  transfers between devices with their start and end apart: 1 -> 1, of which waited for: 0 -> 1; matrix products, arithmetic and copies ran while one was open for 0% -> 0% of each run, Pallas kernels for 42% -> 34%
where the time goes in v2:
time: 39.1 us; the launch traced here: 38.9 us
  Pallas kernels  23.6 us (60%)
  starting transfers between devices  11.5 us (29%)
  waiting for transfers between devices  3.83 us (10%)
    pallas_call x1, Pallas kernels, phases(): pl.pallas_call(phase_kernel, in_specs=[pl.BlockSpec(memory_space=pltpu.HB...  13.4 us
    all_to_all x1, starting transfers between devices, on_device(): got = lax.all_to_all(sent, AXES, 0, 0, tiled=True)  11.5 us
    pallas_call x1, Pallas kernels, levels(): pl.pallas_call(level_kernel, in_specs=[pl.BlockSpec(memory_space=pltpu.VM...  8.07 us
    all_to_all x1, waiting for transfers between devices, on_device(): got = lax.all_to_all(sent, AXES, 0, 0, tiled=True)  3.83 us
    pallas_call x1, Pallas kernels, pack(): pl.pallas_call(pack_kernel, in_specs=[pl.BlockSpec(memory_space=pltpu.HBM...  2.13 us
  transfers between devices with their start and end apart: 1, of which 1 were waited for; matrix products, arithmetic and copies ran while one was open for 0% of the time, Pallas kernels for 34%

profile of v2, /device:TPU:1, one launch (start us, length us, event | category | flops | bytes accessed | tf_op | source)
XLA Modules:
  0.0 38.9 jit_solution(9890701882208266231)
XLA Ops:
  0.0 2.1 %shard_map.55 = f32[1664,128]{1,0:T(8,128)} custom-call(f32[50,32,128]{2,1,0:T(8,128)} %bitcast.10), custom_call_target="tpu_custom_call" | custom-call | flops 1000000 | bytes 1700000 | tf_op jit(solution)/shard_map/pallas_call | solution.py:226
  2.1 11.5 %all-to-all-start = ((f32[128,1,1664]{2,1,0:T(1,128)}), f32[128,1,1664]{2,1,0:T(1,128)S(1)}, u32[]{:S(2)}, u32[]{:S(2)}) async-start(f32[128,1,1664]{2,1,0:T(1,128)} %bitcast.9), calls=%async_computation | async-start | bytes 1703936 | tf_op jit(solution)/shard_map/all_to_all | solution.py:633
  13.7 13.4 %shard_map.56 = (f32[1400,16,128]{2,1,0:T(8,128)}, f32[50,32,128]{2,1,0:T(8,128)}) custom-call(f32[8]{0:T(128)} %amp_hbm.1, f32[2,8]{1,0:T(2,128)} %speed_hbm.1, f32[8]{0:T(128)} %shift_hbm.1, f32[208,128]{1,0:T(8,128)} %constant.2.clone.lane_hbm), custom_call_target="tpu_custom_call" | custom-call | flops 70000000 | bytes 13000000 | tf_op jit(solution)/shard_map/pallas_call | solution.py:416
  27.0 3.8 %all-to-all-done = f32[128,1,1664]{2,1,0:T(1,128)S(1)} async-done(((f32[128,1,1664]{2,1,0:T(1,128)}), f32[128,1,1664]{2,1,0:T(1,128)S(1)}, u32[]{:S(2)}, u32[]{:S(2)}) %all-to-all-start) | async-done | bytes 852000 | tf_op jit(solution)/shard_map/all_to_all | solution.py:633
  30.8 8.1 %shard_map.57 = f32[5,5,64,128]{3,2,1,0:T(8,128)} custom-call(f32[1664,128]{1,0:T(8,128)S(1)} %bitcast.8, f32[1400,16,128]{2,1,0:T(8,128)} %get-tuple-element.7.table_hbm, f32[50,32,128]{2,1,0:T(8,128)} %get-tuple-element.8.first_hbm), custom_call_target="tpu_custom_call" | custom-call | flops 22000000 | bytes 14000000 | tf_op jit(solution)/shard_map/pallas_call | solution.py:603
Async XLA Ops:
  2.1 28.7 %all-to-all-start = ((f32[128,1,1664]{2,1,0:T(1,128)}), f32[128,1,1664]{2,1,0:T(1,128)S(1)}, u32[]{:S(2)}, u32[]{:S(2)}) async-start(f32[128,1,1664]{2,1,0:T(1,128)} %bitcast.9), calls=%async_computation | async-start | bytes 1703936 | tf_op jit(solution)/shard_map/all_to_all | solution.py:633

commit v3 on v2

--- a/solution.py
+++ b/solution.py
@@ -187,22 +187,17 @@
     high = lane >= 2 * LOW
     odd = lane % (2 * LOW) >= LOW
     groups = planes_hbm.shape[1] // 8
-    size = 8 * PACK * PACKED
-    fetches, stores = [], []
-    for g in range(groups):
-        fetches.append(
-            pltpu.make_async_copy(
-                planes_hbm.at[:, pl.ds(8 * g, 8), :], in_ref.at[g], in_sems.at[g]
-            )
-        )
-        part = pl.ds(g * size, size)
-        stores.append(
-            pltpu.make_async_copy(out_ref.at[part], out_hbm.at[part], out_sems.at[g])
-        )
-    for fetch in fetches:
-        fetch.start()
-    for g in range(groups):
-        fetches[g].wait()
+
+    def fetch(g):
+        rows = pl.ds(pl.multiple_of(8 * g, 8), 8)
+        return pltpu.make_async_copy(planes_hbm.at[:, rows, :], in_ref.at[g], in_sems.at[g])
+
+    def store(g):
+        part = pl.ds(pl.multiple_of(g * size, 8), size)
+        return pltpu.make_async_copy(out_ref.at[part], out_hbm.at[part], out_sems.at[g])
+
+    def group_step(g, carry):
+        fetch(g).wait()
         for m in range(PACKED):
             blocks = [in_ref[g, min(PACK * m + n, PLANES - 1)] for n in range(PACK)]
             blocks = [
@@ -216,9 +211,15 @@
                     jnp.where(odd, part[1], part[0]),
                 )
                 out_ref[pl.ds(g * size + r * PACKED + m, 8, stride=PACK * PACKED), :] = turned
-        stores[g].start()
-    for store in stores:
-        store.wait()
+        store(g).start()
+        return carry
+
+    size = 8 * PACK * PACKED
+    for g in range(groups):
+        fetch(g).start()
+    lax.fori_loop(0, groups, group_step, 0)
+    for g in range(groups):
+        store(g).wait()
 
 
 def pack(planes):
@@ -251,13 +252,13 @@
     shift_hbm,
     lane_hbm,
     table_hbm,
-    first_hbm,
+    table0_ref,
+    first_ref,
     amp_ref,
     speed_ref,
     shift_ref,
     lane_ref,
     table_ref,
-    first_ref,
     row_ref,
     wave_ref,
     mode_ref,
@@ -356,14 +357,17 @@
         return carry
 
     lax.fori_loop(0, NODES // 2 + 1, first_step, 0)
-    first_copy = pltpu.make_async_copy(first_ref, first_hbm, sems.at[5])
-    first_copy.start()
 
     def table_copy(level):
-        part = pl.ds(level * LEVEL_TABLE, LEVEL_TABLE)
         return pltpu.make_async_copy(
-            table_ref.at[part], table_hbm.at[part], out_sems.at[level]
+            table_ref.at[pl.ds(level * LEVEL_TABLE, LEVEL_TABLE)],
+            table_hbm.at[pl.ds((level - 1) * LEVEL_TABLE, LEVEL_TABLE)],
+            out_sems.at[level],
         )
+
+    table0_copy = pltpu.make_async_copy(
+        table_ref.at[pl.ds(0, LEVEL_TABLE)], table0_ref, out_sems.at[0]
+    )
 
     def level_step(level, carry):
         top = level * TABLE
@@ -403,12 +407,18 @@
             return inner_carry
 
         lax.fori_loop(0, CHEB, row_step, 0)
+        return carry
+
+    def later_step(level, carry):
+        level_step(level, carry)
         table_copy(level).start()
         return carry
 
-    lax.fori_loop(0, BITS, level_step, 0)
-    first_copy.wait()
-    for level in range(BITS):
+    level_step(0, 0)
+    table0_copy.start()
+    lax.fori_loop(1, BITS, later_step, 0)
+    table0_copy.wait()
+    for level in range(1, BITS):
         table_copy(level).wait()
 
 
@@ -416,10 +426,15 @@
     return pl.pallas_call(
         phase_kernel,
         in_specs=[pl.BlockSpec(memory_space=pltpu.HBM)] * 4,
-        out_specs=[pl.BlockSpec(memory_space=pltpu.HBM)] * 2,
+        out_specs=[
+            pl.BlockSpec(memory_space=pltpu.HBM),
+            pl.BlockSpec(memory_space=pltpu.VMEM),
+            pl.BlockSpec(memory_space=pltpu.VMEM),
+        ],
         out_shape=[
-            pltpu.HBM((BITS * LEVEL_TABLE, HALF, LANES), jnp.float32),
-            pltpu.HBM((2 * NODES, LOW, LANES), jnp.float32),
+            pltpu.HBM(((BITS - 1) * LEVEL_TABLE, HALF, LANES), jnp.float32),
+            pltpu.VMEM((LEVEL_TABLE, HALF, LANES), jnp.float32),
+            pltpu.VMEM((2 * NODES, LOW, LANES), jnp.float32),
         ],
         scratch_shapes=[
             pltpu.SMEM((MODES,), jnp.float32),
@@ -427,7 +442,6 @@
             pltpu.SMEM((MODES,), jnp.float32),
             pltpu.VMEM(lanes.shape, jnp.float32),
             pltpu.VMEM((BITS * LEVEL_TABLE, HALF, LANES), jnp.float32),
-            pltpu.VMEM((2 * NODES, LOW, LANES), jnp.float32),
             pltpu.VMEM((2 * MODES, LOW, LANES), jnp.float32),
             pltpu.VMEM((2 * MODES, HALF, LANES), jnp.float32),
             pltpu.VMEM(((BITS + 1) * 2 * MODES, LANES), jnp.float32),
@@ -445,20 +459,20 @@
 def level_kernel(
     got_ref,
     table_hbm,
-    first_hbm,
+    table0_ref,
+    first_ref,
     out_hbm,
     state_ref,
     other_ref,
     table_ref,
-    first_ref,
     out_ref,
     slot0_ref,
     slot1_ref,
     sems,
     out_sems,
 ):
-    copies = [pltpu.make_async_copy(first_hbm, first_ref, sems.at[BITS])]
-    for level in range(BITS):
+    copies = []
+    for level in range(BITS - 1):
         part = pl.ds(level * LEVEL_TABLE, LEVEL_TABLE)
         copies.append(
             pltpu.make_async_copy(table_hbm.at[part], table_ref.at[part], sems.at[level])
@@ -466,13 +480,22 @@
     for copy in copies:
         copy.start()
     turn = lax.axis_index(AXES) % PACK
-    for m in range(PACKED):
+
+    def unpack(m):
         block = got_ref[pl.ds(m, DEVICES, stride=PACKED), :].T
         for n in range(PACK):
             plane = PACK * m + lax.rem(n + PACK - turn, PACK)
             state_ref[pl.ds(pl.multiple_of(plane * LOW, LOW), LOW), :] = block[
                 n * LOW : (n + 1) * LOW, :
             ]
+
+    def unpack_step(k, carry):
+        for m in range(3):
+            unpack(3 * k + m)
+        return carry
+
+    unpack(PACKED - 1)
+    lax.fori_loop(0, PACKED // 3, unpack_step, 0)
     lane = lax.broadcasted_iota(jnp.int32, (8, LANES), 1)
     order = lane % 2
     for bit in range(1, BITS):
@@ -509,8 +532,10 @@
         def rotated(half, a, near):
             real = imag = None
             for c in range(2):
-                e = 2 * (((2 * level + c) * 2 + half) * NODES + a * CHEB + b)
-                cosine, sine = table_ref[e, rows, :], table_ref[e + 1, rows, :]
+                table = table_ref if level else table0_ref
+                e = 2 * ((2 * c + half) * NODES + a * CHEB + b)
+                e = e + max(level - 1, 0) * LEVEL_TABLE
+                cosine, sine = table[e, rows, :], table[e + 1, rows, :]
                 re, im = near[0][c], near[1][c]
                 new_re, new_im = re * cosine - im * sine, re * sine + im * cosine
                 real = new_re if c == 0 else real + new_re
@@ -576,9 +601,9 @@
     def out_copy(b):
         return pltpu.make_async_copy(out_ref.at[:, b], out_hbm.at[:, b], out_sems.at[b])
 
-    copies[0].wait()
     for level in range(BITS):
-        copies[1 + level].wait()
+        if level:
+            copies[level - 1].wait()
         for t in range(HALF // 8):
             fetch(level, 0, t)
 
@@ -599,32 +624,32 @@
         out_copy(b).wait()
 
 
-def levels(got, table, first):
+def levels(got, table, table0, first):
     return pl.pallas_call(
         level_kernel,
         in_specs=[
             pl.BlockSpec(memory_space=pltpu.VMEM),
             pl.BlockSpec(memory_space=pltpu.HBM),
-            pl.BlockSpec(memory_space=pltpu.HBM),
+            pl.BlockSpec(memory_space=pltpu.VMEM),
+            pl.BlockSpec(memory_space=pltpu.VMEM),
         ],
         out_specs=pl.BlockSpec(memory_space=pltpu.HBM),
         out_shape=pltpu.HBM((CHEB, CHEB, 2 * LOW, LANES), jnp.float32),
         scratch_shapes=[
             pltpu.VMEM((PACK * PACKED * LOW, LANES), jnp.float32),
             pltpu.VMEM((PLANES * LOW, LANES), jnp.float32),
-            pltpu.VMEM((BITS * LEVEL_TABLE, HALF, LANES), jnp.float32),
-            pltpu.VMEM((2 * NODES, LOW, LANES), jnp.float32),
+            pltpu.VMEM(((BITS - 1) * LEVEL_TABLE, HALF, LANES), jnp.float32),
             pltpu.VMEM((CHEB, CHEB, 2 * LOW, LANES), jnp.float32),
             pltpu.VMEM((4 * CHEB, 8, LANES), jnp.float32),
             pltpu.VMEM((4 * CHEB, 8, LANES), jnp.float32),
-            pltpu.SemaphoreType.DMA((BITS + 1,)),
+            pltpu.SemaphoreType.DMA((BITS - 1,)),
             pltpu.SemaphoreType.DMA((CHEB,)),
         ],
         compiler_params=pltpu.CompilerParams(vmem_limit_bytes=32 * 2**20),
         cost_estimate=pl.CostEstimate(
             flops=22 * 10**6, bytes_accessed=14 * 10**6, transcendentals=0
         ),
-    )(got, in_hbm(table), in_hbm(first))
+    )(got, in_hbm(table), table0, first)
 
 
 def on_device(coefficients, speed_amp, speed_wave, speed_shift):
@@ -632,8 +657,8 @@
     sent = packed.reshape(DEVICES, 1, PACKED * LANES)
     got = lax.all_to_all(sent, AXES, 0, 0, tiled=True)
     got = got.reshape(DEVICES * PACKED, LANES)
-    table, first = phases(speed_amp, speed_wave, speed_shift, jnp.asarray(lane_tables()))
-    final = levels(got, table, first).reshape(CHEB, CHEB, LOW, 2, LANES)
+    table, table0, first = phases(speed_amp, speed_wave, speed_shift, jnp.asarray(lane_tables()))
+    final = levels(got, table, table0, first).reshape(CHEB, CHEB, LOW, 2, LANES)
     return final.transpose(3, 0, 1, 2, 4).reshape(2, CHEB, CHEB, LOW * LANES)
 
 

time: 39.1 us -> 38.1 us (0.974)
  Pallas kernels: 23.6 us -> 22.8 us
    pallas_call x1, Pallas kernels: 8.07 us -> 7.08 us  [levels(): pl.pallas_call(level_kernel, in_specs=[pl.BlockSpec(memory_space=pltpu.VM...]
  transfers between devices with their start and end apart: 1 -> 1, of which waited for: 1 -> 1; matrix products, arithmetic and copies ran while one was open for 0% -> 0% of each run, Pallas kernels for 34% -> 36%
where the time goes in v3:
time: 38.1 us; the launch traced here: 37.9 us
  Pallas kernels  22.8 us (60%)
  starting transfers between devices  11.5 us (30%)
  waiting for transfers between devices  3.63 us (10%)
    pallas_call x1, Pallas kernels, phases(): pl.pallas_call(phase_kernel, in_specs=[pl.BlockSpec(memory_space=pltpu.HB...  13.6 us
    all_to_all x1, starting transfers between devices, on_device(): got = lax.all_to_all(sent, AXES, 0, 0, tiled=True)  11.5 us
    pallas_call x1, Pallas kernels, levels(): pl.pallas_call(level_kernel, in_specs=[pl.BlockSpec(memory_space=pltpu.VM...  7.08 us
    all_to_all x1, waiting for transfers between devices, on_device(): got = lax.all_to_all(sent, AXES, 0, 0, tiled=True)  3.63 us
    pallas_call x1, Pallas kernels, pack(): pl.pallas_call(pack_kernel, in_specs=[pl.BlockSpec(memory_space=pltpu.HBM...  2.14 us
  transfers between devices with their start and end apart: 1, of which 1 were waited for; matrix products, arithmetic and copies ran while one was open for 0% of the time, Pallas kernels for 36%

profile of v3, /device:TPU:1, one launch (start us, length us, event | category | flops | bytes accessed | tf_op | source)
XLA Modules:
  0.0 37.9 jit_solution(1264345162454171748)
XLA Ops:
  0.0 2.1 %shard_map.55 = f32[1664,128]{1,0:T(8,128)} custom-call(f32[50,32,128]{2,1,0:T(8,128)} %bitcast.10), custom_call_target="tpu_custom_call" | custom-call | flops 1000000 | bytes 1700000 | tf_op jit(solution)/shard_map/pallas_call | solution.py:227
  2.1 11.5 %all-to-all-start = ((f32[128,1,1664]{2,1,0:T(1,128)}), f32[128,1,1664]{2,1,0:T(1,128)S(1)}, u32[]{:S(2)}, u32[]{:S(2)}) async-start(f32[128,1,1664]{2,1,0:T(1,128)} %bitcast.9), calls=%async_computation | async-start | bytes 1703936 | tf_op jit(solution)/shard_map/all_to_all | solution.py:658
  13.7 13.6 %shard_map.56 = (f32[1200,16,128]{2,1,0:T(8,128)}, f32[200,16,128]{2,1,0:T(8,128)S(1)}, f32[50,32,128]{2,1,0:T(8,128)S(1)}) custom-call(f32[8]{0:T(128)} %amp_hbm.1, f32[2,8]{1,0:T(2,128)} %speed_hbm.1, f32[8]{0:T(128)} %shift_hbm.1, f32[208,128]{1,0:T(8,128)} %constant.2.clone.lane_hbm), custom_call_target="tpu_custom_call" | custom-call | flops 70000000 | bytes 13000000 | tf_op jit(solution)/shard_map/pallas_call | solution.py:426
  27.2 3.6 %all-to-all-done = f32[128,1,1664]{2,1,0:T(1,128)S(1)} async-done(((f32[128,1,1664]{2,1,0:T(1,128)}), f32[128,1,1664]{2,1,0:T(1,128)S(1)}, u32[]{:S(2)}, u32[]{:S(2)}) %all-to-all-start) | async-done | bytes 852000 | tf_op jit(solution)/shard_map/all_to_all | solution.py:658
  30.8 7.1 %shard_map.57 = f32[5,5,64,128]{3,2,1,0:T(8,128)} custom-call(f32[1664,128]{1,0:T(8,128)S(1)} %bitcast.8, f32[1200,16,128]{2,1,0:T(8,128)} %get-tuple-element.8.table_hbm, f32[200,16,128]{2,1,0:T(8,128)S(1)} %get-tuple-element.9.table0_ref, f32[50,32,128]{2,1,0:T(8,128)S(1)} %get-tuple-element.10.first_ref), custom_call_target="tpu_custom_call" | custom-call | flops 22000000 | bytes 14000000 | tf_op jit(solution)/shard_map/pallas_call | solution.py:628
Async XLA Ops:
  2.1 28.7 %all-to-all-start = ((f32[128,1,1664]{2,1,0:T(1,128)}), f32[128,1,1664]{2,1,0:T(1,128)S(1)}, u32[]{:S(2)}, u32[]{:S(2)}) async-start(f32[128,1,1664]{2,1,0:T(1,128)} %bitcast.9), calls=%async_computation | async-start | bytes 1703936 | tf_op jit(solution)/shard_map/all_to_all | solution.py:658

commit v4 on v3

--- a/solution.py
+++ b/solution.py
@@ -173,9 +173,11 @@
 
 
 def swap(left, right, shift, low):
-    first = jnp.where(low, left, pltpu.roll(right, shift, 1))
-    second = jnp.where(low, pltpu.roll(left, LANES - shift, 1), right)
-    return first, second
+    lane = lax.broadcasted_iota(jnp.int32, left.shape, 1)
+    moved = jnp.take_along_axis(
+        jnp.where(low, right, left), jnp.bitwise_xor(lane, shift), axis=1
+    )
+    return jnp.where(low, left, moved), jnp.where(low, moved, right)
 
 
 def in_hbm(value):

time: 38.1 us -> 37.5 us (0.984)
  Pallas kernels: 22.8 us -> 22.1 us
    pallas_call x1, Pallas kernels: 7.08 us -> 6.42 us  [levels(): pl.pallas_call(level_kernel, in_specs=[pl.BlockSpec(memory_space=pltpu.VM...]
where the time goes in v4:
time: 37.5 us; the launch traced here: 37.3 us
  Pallas kernels  22.1 us (59%)
  starting transfers between devices  11.5 us (31%)
  waiting for transfers between devices  3.63 us (10%)
    pallas_call x1, Pallas kernels, phases(): pl.pallas_call(phase_kernel, in_specs=[pl.BlockSpec(memory_space=pltpu.HB...  13.6 us
    all_to_all x1, starting transfers between devices, on_device(): got = lax.all_to_all(sent, AXES, 0, 0, tiled=True)  11.5 us
    pallas_call x1, Pallas kernels, levels(): pl.pallas_call(level_kernel, in_specs=[pl.BlockSpec(memory_space=pltpu.VM...  6.42 us
    all_to_all x1, waiting for transfers between devices, on_device(): got = lax.all_to_all(sent, AXES, 0, 0, tiled=True)  3.63 us
    pallas_call x1, Pallas kernels, pack(): pl.pallas_call(pack_kernel, in_specs=[pl.BlockSpec(memory_space=pltpu.HBM...  2.14 us
  transfers between devices with their start and end apart: 1, of which 1 were waited for; matrix products, arithmetic and copies ran while one was open for 0% of the time, Pallas kernels for 36%

profile of v4, /device:TPU:1, one launch (start us, length us, event | category | flops | bytes accessed | tf_op | source)
XLA Modules:
  0.0 37.3 jit_solution(18049719674165127845)
XLA Ops:
  0.0 2.1 %shard_map.55 = f32[1664,128]{1,0:T(8,128)} custom-call(f32[50,32,128]{2,1,0:T(8,128)} %bitcast.10), custom_call_target="tpu_custom_call" | custom-call | flops 1000000 | bytes 1700000 | tf_op jit(solution)/shard_map/pallas_call | solution.py:229
  2.1 11.5 %all-to-all-start = ((f32[128,1,1664]{2,1,0:T(1,128)}), f32[128,1,1664]{2,1,0:T(1,128)S(1)}, u32[]{:S(2)}, u32[]{:S(2)}) async-start(f32[128,1,1664]{2,1,0:T(1,128)} %bitcast.9), calls=%async_computation | async-start | bytes 1703936 | tf_op jit(solution)/shard_map/all_to_all | solution.py:660
  13.7 13.6 %shard_map.56 = (f32[1200,16,128]{2,1,0:T(8,128)}, f32[200,16,128]{2,1,0:T(8,128)S(1)}, f32[50,32,128]{2,1,0:T(8,128)S(1)}) custom-call(f32[8]{0:T(128)} %amp_hbm.1, f32[2,8]{1,0:T(2,128)} %speed_hbm.1, f32[8]{0:T(128)} %shift_hbm.1, f32[208,128]{1,0:T(8,128)} %constant.2.clone.lane_hbm), custom_call_target="tpu_custom_call" | custom-call | flops 70000000 | bytes 13000000 | tf_op jit(solution)/shard_map/pallas_call | solution.py:428
  27.2 3.6 %all-to-all-done = f32[128,1,1664]{2,1,0:T(1,128)S(1)} async-done(((f32[128,1,1664]{2,1,0:T(1,128)}), f32[128,1,1664]{2,1,0:T(1,128)S(1)}, u32[]{:S(2)}, u32[]{:S(2)}) %all-to-all-start) | async-done | bytes 852000 | tf_op jit(solution)/shard_map/all_to_all | solution.py:660
  30.8 6.4 %shard_map.57 = f32[5,5,64,128]{3,2,1,0:T(8,128)} custom-call(f32[1664,128]{1,0:T(8,128)S(1)} %bitcast.8, f32[1200,16,128]{2,1,0:T(8,128)} %get-tuple-element.8.table_hbm, f32[200,16,128]{2,1,0:T(8,128)S(1)} %get-tuple-element.9.table0_ref, f32[50,32,128]{2,1,0:T(8,128)S(1)} %get-tuple-element.10.first_ref), custom_call_target="tpu_custom_call" | custom-call | flops 22000000 | bytes 14000000 | tf_op jit(solution)/shard_map/pallas_call | solution.py:630
Async XLA Ops:
  2.1 28.7 %all-to-all-start = ((f32[128,1,1664]{2,1,0:T(1,128)}), f32[128,1,1664]{2,1,0:T(1,128)S(1)}, u32[]{:S(2)}, u32[]{:S(2)}) async-start(f32[128,1,1664]{2,1,0:T(1,128)} %bitcast.9), calls=%async_computation | async-start | bytes 1703936 | tf_op jit(solution)/shard_map/all_to_all | solution.py:660

commit v5 on v4

--- a/solution.py
+++ b/solution.py
@@ -334,8 +334,10 @@
             sums.append((x + y, x - y))
         return tuple(sums)
 
-    def put(ref, at, rows, turns):
+    def put(ref, at, rows, turns, scale=None):
         sine, cosine = sin_cos(turns)
+        if scale is not None:
+            sine, cosine = sine * scale, cosine * scale
         ref[at, rows, :] = cosine
         ref[at + 1, rows, :] = sine
 
@@ -388,7 +390,12 @@
             for here, there in differences(wave_ref, level, NODES // 2, HALF // 8)
         ]
 
+        _, child = points_of()
+
         def row_step(a, inner_carry):
+            scale = jnp.float32(1.0)
+            for i in range(1, CHEB - 1):
+                scale = jnp.where(a == i, float(lagrange_of(child[0, i])[2]), scale)
             lines = [
                 (
                     lane_ref[pl.ds(top + 5 + 2 * CHEB * c + a, 1), :],
@@ -405,7 +412,7 @@
                         rows = slice(8 * t, 8 * t + 8)
                         for k, place in enumerate((2 * p, 2 * (2 * NODES - 1 - p))):
                             turns = far[t][k] * apart[c] + (moved[t][k] + lines[c][k])
-                            put(table_ref, at + place, rows, turns)
+                            put(table_ref, at + place, rows, turns, scale)
             return inner_carry
 
         lax.fori_loop(0, CHEB, row_step, 0)
@@ -579,6 +586,7 @@
         held = {}
         for i in range(1, CHEB - 1):
             row = lagrange_of(child[0, i])
+            row = row / row[2]
             sums, gaps = [[], []], [[], []]
             for r in range(2):
                 for c in range(2):
@@ -586,7 +594,7 @@
                     even = (
                         float((row[0] + row[4]) / 2) * even0
                         + float((row[1] + row[3]) / 2) * even1
-                        + float(row[2]) * middle
+                        + middle
                     )
                     odd = (
                         float((row[0] - row[4]) / 2) * odd0

time: 37.5 us -> 37.4 us (level)
  waiting for transfers between devices: 3.63 us -> 3.22 us
    pallas_call x1, Pallas kernels: 13.6 us -> 14 us  [phases(): pl.pallas_call(phase_kernel, in_specs=[pl.BlockSpec(memory_space=pltpu.HB...]
    all_to_all x1, waiting for transfers between devices: 3.63 us -> 3.22 us  [on_device(): got = lax.all_to_all(sent, AXES, 0, 0, tiled=True)]
  transfers between devices with their start and end apart: 1 -> 1, of which waited for: 1 -> 1; matrix products, arithmetic and copies ran while one was open for 0% -> 0% of each run, Pallas kernels for 36% -> 38%
where the time goes in v5:
time: 37.4 us; the launch traced here: 37.2 us
  Pallas kernels  22.4 us (60%)
  starting transfers between devices  11.5 us (31%)
  waiting for transfers between devices  3.22 us (9%)
    pallas_call x1, Pallas kernels, phases(): pl.pallas_call(phase_kernel, in_specs=[pl.BlockSpec(memory_space=pltpu.HB...  14 us
    all_to_all x1, starting transfers between devices, on_device(): got = lax.all_to_all(sent, AXES, 0, 0, tiled=True)  11.5 us
    pallas_call x1, Pallas kernels, levels(): pl.pallas_call(level_kernel, in_specs=[pl.BlockSpec(memory_space=pltpu.VM...  6.34 us
    all_to_all x1, waiting for transfers between devices, on_device(): got = lax.all_to_all(sent, AXES, 0, 0, tiled=True)  3.22 us
    pallas_call x1, Pallas kernels, pack(): pl.pallas_call(pack_kernel, in_specs=[pl.BlockSpec(memory_space=pltpu.HBM...  2.14 us
  transfers between devices with their start and end apart: 1, of which 1 were waited for; matrix products, arithmetic and copies ran while one was open for 0% of the time, Pallas kernels for 38%

profile of v5, /device:TPU:1, one launch (start us, length us, event | category | flops | bytes accessed | tf_op | source)
XLA Modules:
  0.0 37.2 jit_solution(9772777670579741959)
XLA Ops:
  0.0 2.1 %shard_map.55 = f32[1664,128]{1,0:T(8,128)} custom-call(f32[50,32,128]{2,1,0:T(8,128)} %bitcast.10), custom_call_target="tpu_custom_call" | custom-call | flops 1000000 | bytes 1700000 | tf_op jit(solution)/shard_map/pallas_call | solution.py:229
  2.1 11.5 %all-to-all-start = ((f32[128,1,1664]{2,1,0:T(1,128)}), f32[128,1,1664]{2,1,0:T(1,128)S(1)}, u32[]{:S(2)}, u32[]{:S(2)}) async-start(f32[128,1,1664]{2,1,0:T(1,128)} %bitcast.9), calls=%async_computation | async-start | bytes 1703936 | tf_op jit(solution)/shard_map/all_to_all | solution.py:668
  13.7 14.0 %shard_map.56 = (f32[1200,16,128]{2,1,0:T(8,128)}, f32[200,16,128]{2,1,0:T(8,128)S(1)}, f32[50,32,128]{2,1,0:T(8,128)S(1)}) custom-call(f32[8]{0:T(128)} %amp_hbm.1, f32[2,8]{1,0:T(2,128)} %speed_hbm.1, f32[8]{0:T(128)} %shift_hbm.1, f32[208,128]{1,0:T(8,128)} %constant.2.clone.lane_hbm), custom_call_target="tpu_custom_call" | custom-call | flops 70000000 | bytes 13000000 | tf_op jit(solution)/shard_map/pallas_call | solution.py:435
  27.6 3.2 %all-to-all-done = f32[128,1,1664]{2,1,0:T(1,128)S(1)} async-done(((f32[128,1,1664]{2,1,0:T(1,128)}), f32[128,1,1664]{2,1,0:T(1,128)S(1)}, u32[]{:S(2)}, u32[]{:S(2)}) %all-to-all-start) | async-done | bytes 852000 | tf_op jit(solution)/shard_map/all_to_all | solution.py:668
  30.8 6.3 %shard_map.57 = f32[5,5,64,128]{3,2,1,0:T(8,128)} custom-call(f32[1664,128]{1,0:T(8,128)S(1)} %bitcast.8, f32[1200,16,128]{2,1,0:T(8,128)} %get-tuple-element.8.table_hbm, f32[200,16,128]{2,1,0:T(8,128)S(1)} %get-tuple-element.9.table0_ref, f32[50,32,128]{2,1,0:T(8,128)S(1)} %get-tuple-element.10.first_ref), custom_call_target="tpu_custom_call" | custom-call | flops 22000000 | bytes 14000000 | tf_op jit(solution)/shard_map/pallas_call | solution.py:638
Async XLA Ops:
  2.1 28.7 %all-to-all-start = ((f32[128,1,1664]{2,1,0:T(1,128)}), f32[128,1,1664]{2,1,0:T(1,128)S(1)}, u32[]{:S(2)}, u32[]{:S(2)}) async-start(f32[128,1,1664]{2,1,0:T(1,128)} %bitcast.9), calls=%async_computation | async-start | bytes 1703936 | tf_op jit(solution)/shard_map/all_to_all | solution.py:668
